TPU v7x, 32 devices: a whole 2x2x4 slice. The times are simulated.
32 devices in a mesh: cam: 8 (over y, x, core), fsdp: 4 (over z).
Axes of the slice: x: 2, y: 2, z: 4, core: 2. Of those that a mesh axis runs over, the one named last changes fastest.
Arguments:
- queries: bfloat16 [4, 1280, 4096], P('fsdp', 'cam'), may hold values from -16 to 16
- keys: bfloat16 [4, 1280, 4096], P('fsdp', 'cam'), may hold values from -16 to 16
- values: bfloat16 [4, 1280, 4096], P('fsdp', 'cam'), may hold values from -6 to 6
- out_weight: bfloat16 [4096, 5120], P('fsdp'), may hold values from -0.09375 to 0.09375
- block_counts: int32 [4, 8], P('fsdp', 'cam'), may hold values from 1 to 5, as said below
- row_mask: int32 [4, 1280], P('fsdp', 'cam'), may hold values from 0 to 1, as said below
Outputs:
- projected: bfloat16 [4, 1280, 5120], P('fsdp', 'cam')
Inputs may be any that keep to these rules, and one draw needn't show every extreme that they name: `block_counts`: every view uses at least one block; in every clip one view uses all 5 blocks. `row_mask`: 0 or 1; the first two rows of every block are 1.
All inputs are finite; a program needn't handle non-finite values.
Results may differ from a plain program's by a relative error of at most 0.0057.
Values may be sent and summed in bfloat16 or wider, within the bound.
No kernel may reach another device: no remote copies, remote signals or barrier semaphores. Data moves between devices by JAX's collectives and lax.ppermute only.
A program may use at most 128 MiB of HBM per device.

v0:
```python
import math

import jax
import jax.numpy as jnp
from jax import lax
from jax.sharding import PartitionSpec as P

HEAD_DIM = 128
BLOCK = 32


def attend(query_rows, key_rows, value_rows, key_ok):
    score_scale = 1.0 / math.sqrt(HEAD_DIM)
    count_all = query_rows.shape[0]
    head_count = query_rows.shape[1] // HEAD_DIM
    block_rows = 512 if count_all % 512 == 0 else count_all
    outputs = []
    for head_number in range(head_count):
        column = head_number * HEAD_DIM
        query_h = query_rows[:, column : column + HEAD_DIM].reshape(
            count_all // block_rows, block_rows, HEAD_DIM
        )
        key_h = key_rows[:, column : column + HEAD_DIM]
        value_h = value_rows[:, column : column + HEAD_DIM]

        def one_block(query_block):
            scores = (
                jnp.einsum("qd,kd->qk", query_block, key_h, preferred_element_type=jnp.float32)
                * score_scale
            )
            scores = jnp.where(key_ok[None, :], scores, jnp.float32(-1e30))
            row_top = jnp.max(scores, axis=1, keepdims=True)
            raised = jnp.exp(scores - row_top)
            weights = (raised / jnp.sum(raised, axis=1, keepdims=True)).astype(jnp.bfloat16)
            return jnp.dot(weights, value_h, preferred_element_type=jnp.float32).astype(
                jnp.bfloat16
            )

        outputs.append(lax.map(one_block, query_h).reshape(count_all, HEAD_DIM))
    return jnp.concatenate(outputs, axis=1)


def local(queries, keys, values, out_weight, block_counts, row_mask):
    query_rows = queries[0]
    row_count = query_rows.shape[0]
    cam_count = lax.axis_size("cam")
    offsets = jnp.arange(row_count, dtype=jnp.int32)
    row_valid = (row_mask[0] == 1) & (offsets // BLOCK < block_counts[0, 0])
    key_flag = jnp.broadcast_to(row_valid.astype(jnp.bfloat16)[:, None], (row_count, cam_count))
    query_all, key_all, value_all, flag_all = (
        lax.all_to_all(query_rows, "cam", split_axis=1, concat_axis=0, tiled=True),
        lax.all_to_all(keys[0], "cam", split_axis=1, concat_axis=0, tiled=True),
        lax.all_to_all(values[0], "cam", split_axis=1, concat_axis=0, tiled=True),
        lax.all_to_all(key_flag, "cam", split_axis=1, concat_axis=0, tiled=True),
    )
    head_rows = attend(query_all, key_all, value_all, flag_all[:, 0] > 0.5)
    attended = lax.all_to_all(head_rows, "cam", split_axis=0, concat_axis=1, tiled=True)
    columns_all = lax.all_to_all(attended, "fsdp", split_axis=1, concat_axis=0, tiled=True)
    projected = lax.psum_scatter(
        jnp.dot(columns_all, out_weight, preferred_element_type=jnp.float32),
        "fsdp",
        scatter_dimension=0,
        tiled=True,
    )
    result = jnp.where(row_valid[:, None], projected, jnp.float32(0.0)).astype(jnp.bfloat16)
    return result[None]


def solution(mesh):
    in_specs = (
        P("fsdp", "cam", None),
        P("fsdp", "cam", None),
        P("fsdp", "cam", None),
        P("fsdp", None),
        P("fsdp", "cam"),
        P("fsdp", "cam"),
    )
    out_specs = P("fsdp", "cam", None)
    return jax.shard_map(local, mesh=mesh, in_specs=in_specs, out_specs=out_specs, check_vma=False)
```

profile of v0, /device:TPU:0, one launch (start us, length us, event | category | flops | bytes accessed | tf_op | source)
XLA Modules:
  0.0 399.7 jit_solution(11378647031319918467)
XLA Ops:
  7.3 0.7 compare_reduce_fusion
  8.0 0.6 broadcast_in_dim.96
  8.6 5.2 %all-to-all-start = ((bf16[160,8,1]{0,2,1:T(2,128)(2,1)}), bf16[160,8,1]{0,2,1:T(2,128)(2,1)S(1)}, u32[]{:S(2)}, u32[]{:S(2)}) async-start(bf16[160,8,1]{0,2,1:T(2,128)(2,1)} %broadcast_in_dim.96), calls=%async_computation | async-start | bytes 16384 | tf_op jit(solution)/shard_map/all_to_all | solution.py:54
  13.8 1.8 copy.25
  15.6 1.5 copy.20
  17.1 1.4 all-to-all-done
  18.5 3.6 all-to-all-start.1
  22.1 0.0 copy-done.3
  22.1 0.5 copy.26
  22.6 1.5 copy.21
  24.1 16.2 %all-to-all-done.1 = bf16[160,8,512]{2,0,1:T(8,128)(2,1)S(1)} async-done(((bf16[160,8,512]{2,0,1:T(8,128)(2,1)}), bf16[160,8,512]{2,0,1:T(8,128)(2,1)S(1)}, u32[]{:S(2)}, u32[]{:S(2)}) %all-to-all-start.1) | async-done | bytes 1310752 | tf_op jit(solution)/shard_map/all_to_all | solution.py:51
  40.2 3.6 all-to-all-start.2
  43.8 1.8 copy.27
  45.6 1.5 copy.22
  47.1 0.1 gt.19
  47.2 14.7 %all-to-all-done.2 = bf16[160,8,512]{2,0,1:T(8,128)(2,1)S(1)} async-done(((bf16[160,8,512]{2,0,1:T(8,128)(2,1)}), bf16[160,8,512]{2,0,1:T(8,128)(2,1)S(1)}, u32[]{:S(2)}, u32[]{:S(2)}) %all-to-all-start.2) | async-done | bytes 1310752 | tf_op jit(solution)/shard_map/all_to_all | solution.py:52
  61.9 4.3 %all-to-all-start.3 = ((bf16[160,8,512]{2,0,1:T(8,128)(2,1)}), bf16[160,8,512]{2,0,1:T(8,128)(2,1)}, u32[]{:S(2)}, u32[]{:S(2)}) async-start(bf16[160,8,512]{2,0,1:T(8,128)(2,1)} %copy.22), calls=%async_computation.3 | async-start | bytes 2621440 | tf_op jit(solution)/shard_map/all_to_all | solution.py:53
  66.2 0.0 reduce-scatter.2.cloned.1.call-start
  66.3 1.1 fusion.30
  67.4 0.0 copy-start
  67.4 4.1 %fusion.31 = (f32[1280]{0:T(1024)S(1)}, f32[1280,1280]{0,1:T(8,128)}) fusion(bf16[1280,512]{1,0:T(8,128)(2,1)S(1)} %bitcast.45, bf16[1280,512]{1,0:T(8,128)(2,1)S(1)} %bitcast.41, pred[1280]{0:T(1024)(128)(4,1)S(1)} %gt.19), kind=kOutput, calls=%fused_computation.52 | convolution fusion | flops 424344320 | bytes 7216128 | tf_op jit(solution)/shard_map/while/body/eval_jaxpr/qd,kd->qk/dot_general | solution.py:28
  71.5 1.0 fusion.7
  72.5 0.0 copy-done.1
  72.5 0.0 copy-done.2
  72.5 3.5 fusion.32
  76.0 5.1 %fusion.33 = (f32[1280]{0:T(1024)S(1)}, f32[1280,1280]{0,1:T(8,128)}) fusion(bf16[1280,512]{1,0:T(8,128)(2,1)} %bitcast.47, bf16[1280,512]{1,0:T(8,128)(2,1)} %bitcast.43, pred[1280]{0:T(1024)(128)(4,1)S(1)} %gt.19), kind=kOutput, calls=%fused_computation.54 | convolution fusion | flops 424344320 | bytes 7215360 | tf_op jit(solution)/shard_map/while/body/eval_jaxpr/qd,kd->qk/dot_general | solution.py:28
  81.0 3.4 all-to-all-done.3
  84.5 4.3 %fusion.12 = bf16[1280,128]{1,0:T(8,128)(2,1)S(1)} fusion(f32[1280,1280]{0,1:T(8,128)} %copy-done, f32[1280]{0:T(1024)S(1)} %fusion.7, f32[1280]{0:T(1024)S(1)} %get-tuple-element.53, bf16[1280,512]{1,0:T(8,128)(2,1)} %bitcast.7), kind=kOutput, calls=%fused_computation.25 | convolution fusion | flops 424509440 | bytes 7219200 | tf_op jit(solution)/shard_map/while/body/eval_jaxpr/dot_general | solution.py:35
  88.7 0.0 slice-start.2
  88.8 0.9 fusion.6
  89.7 2.5 fusion.13
  92.3 0.0 slice-done.2
  92.3 0.0 slice-done.3
  92.3 0.0 slice-start
  92.3 1.0 fusion.5
  93.3 2.5 fusion.14
  95.8 1.0 fusion.4
  96.8 2.2 fusion.15
  99.0 0.1 pad_maximum_fusion
  99.2 20.6 %all_to_all.99 = bf16[8,160,512]{2,1,0:T(8,128)(2,1)S(1)} all-to-all(bf16[8,160,512]{2,1,0:T(8,128)(2,1)S(1)} %pad_maximum_fusion), channel_id=1, replica_groups=mesh['cam'=8,'fsdp'=4] {'cam'}, dimensions={0} | all-to-all | bytes 2621440 | tf_op jit(solution)/shard_map/all_to_all | solution.py:57
  119.8 0.7 copy.23
  120.5 0.9 all_to_all.89
  121.4 0.4 copy.24
  121.8 35.4 %all_to_all.100 = bf16[160,4,1024]{2,0,1:T(8,128)(2,1)S(1)} all-to-all(bf16[160,4,1024]{2,0,1:T(8,128)(2,1)S(1)} %copy.24), channel_id=1, replica_groups=mesh['cam'=8,'fsdp'=4] {'fsdp'}, dimensions={1} | all-to-all | bytes 2621440 | tf_op jit(solution)/shard_map/all_to_all | solution.py:58
  157.2 13.8 %fusion.34 = f32[640,5120]{1,0:T(8,128)} fusion(bf16[640,1024]{1,0:T(8,128)(2,1)S(1)} %bitcast.55, bf16[1024,5120]{1,0:T(8,128)(2,1)} %param.9), kind=kOutput, calls=%fused_computation.55 | convolution fusion | flops 6710886400 | bytes 24903680 | tf_op jit(solution)/shard_map/dot_general | solution.py:60
  171.0 0.0 reduce-scatter.2.cloned.1.call-update
  171.1 218.4 %reduce-scatter.2.cloned.1.call-done = f32[160,5120]{1,0:T(8,128)} async-done(((f32[640,5120]{1,0:T(8,128)}), f32[160,5120]{1,0:T(8,128)}) %reduce-scatter.2.cloned.1.call-update) | async-done | bytes 3276816 | tf_op jit(solution)/shard_map/reduce_scatter | solution.py:59
  389.5 3.4 fusion.16
  (17 shorter events, 0.1 us)
Async XLA Ops:
  6.5 15.5 %copy-start.3 = (bf16[1,160,4096]{2,1,0:T(8,128)(2,1)S(1)}, bf16[1,160,4096]{2,1,0:T(8,128)(2,1)}, u32[]{:S(2)}) copy-start(bf16[1,160,4096]{2,1,0:T(8,128)(2,1)} %param.7) | copy-start | bytes 3932164
  8.6 9.9 %all-to-all-start = ((bf16[160,8,1]{0,2,1:T(2,128)(2,1)}), bf16[160,8,1]{0,2,1:T(2,128)(2,1)S(1)}, u32[]{:S(2)}, u32[]{:S(2)}) async-start(bf16[160,8,1]{0,2,1:T(2,128)(2,1)} %broadcast_in_dim.96), calls=%async_computation | async-start | bytes 16384 | tf_op jit(solution)/shard_map/all_to_all | solution.py:54
  18.5 21.7 %all-to-all-start.1 = ((bf16[160,8,512]{2,0,1:T(8,128)(2,1)}), bf16[160,8,512]{2,0,1:T(8,128)(2,1)S(1)}, u32[]{:S(2)}, u32[]{:S(2)}) async-start(bf16[160,8,512]{2,0,1:T(8,128)(2,1)} %copy.20), calls=%async_computation.1 | async-start | bytes 2621440 | tf_op jit(solution)/shard_map/all_to_all | solution.py:51
  40.2 32.3 %copy-start.1 = (bf16[160,8,512]{2,0,1:T(8,128)(2,1)}, bf16[160,8,512]{2,0,1:T(8,128)(2,1)S(1)}, u32[]{:S(2)}) copy-start(bf16[160,8,512]{2,0,1:T(8,128)(2,1)S(1)} %all-to-all-done.1) | copy-start | bytes 3932164
  40.2 21.7 %all-to-all-start.2 = ((bf16[160,8,512]{2,0,1:T(8,128)(2,1)}), bf16[160,8,512]{2,0,1:T(8,128)(2,1)S(1)}, u32[]{:S(2)}, u32[]{:S(2)}) async-start(bf16[160,8,512]{2,0,1:T(8,128)(2,1)} %copy.21), calls=%async_computation.2 | async-start | bytes 2621440 | tf_op jit(solution)/shard_map/all_to_all | solution.py:52
  61.9 10.5 %copy-start.2 = (bf16[160,8,512]{2,0,1:T(8,128)(2,1)}, bf16[160,8,512]{2,0,1:T(8,128)(2,1)S(1)}, u32[]{:S(2)}) copy-start(bf16[160,8,512]{2,0,1:T(8,128)(2,1)S(1)} %all-to-all-done.2) | copy-start | bytes 3932164
  61.9 22.5 %all-to-all-start.3 = ((bf16[160,8,512]{2,0,1:T(8,128)(2,1)}), bf16[160,8,512]{2,0,1:T(8,128)(2,1)}, u32[]{:S(2)}, u32[]{:S(2)}) async-start(bf16[160,8,512]{2,0,1:T(8,128)(2,1)} %copy.22), calls=%async_computation.3 | async-start | bytes 2621440 | tf_op jit(solution)/shard_map/all_to_all | solution.py:53
  66.2 323.3 %reduce-scatter.2.cloned.1.call-start = ((), (), s32[]{:S(2)}) async-start(), calls=%async_computation.7 | async-start | bytes 16384000 | tf_op jit(solution)/shard_map/reduce_scatter | solution.py:59
  67.4 5.1 %copy-start = (f32[1280,1280]{0,1:T(8,128)}, f32[1280,1280]{0,1:T(8,128)S(1)}, u32[]{:S(2)}) copy-start(f32[1280,1280]{0,1:T(8,128)S(1)} %get-tuple-element.60) | copy-start | bytes 19660804
  76.0 12.7 %slice-start.4 = ((s8[6553600]{0:T(1024)(128)(4,1)}), s8[2359296]{0:T(1024)(128)(4,1)S(1)}, s32[]{:S(2)}) async-start(s8[6553600]{0:T(1024)(128)(4,1)} %bitcast.38), calls=%async_computation.12 | async-start | bytes 4718592
  84.5 4.3 %slice-start.5 = ((s8[6553600]{0:T(1024)(128)(4,1)}), s8[4194304]{0:T(1024)(128)(4,1)S(1)}, s32[]{:S(2)}) async-start(s8[6553600]{0:T(1024)(128)(4,1)} %bitcast.38), calls=%async_computation.13 | async-start | bytes 8388608
  88.7 3.5 slice-start.2
  89.7 2.6 slice-start.3
  92.3 3.5 slice-start
  93.3 2.5 slice-start.1
Sparse Core Ops, SparseCore 0:
  171.2 218.2 reduce-scatter.1
where the time goes:
time: 400 us
  waiting for transfers between devices  254 us (64%)
  blocking collectives  56 us (14%)
  matrix products  39.1 us (10%)
  starting transfers between devices  16.6 us (4%)
  between operations  14.4 us (4%)
  local copies, waits for them, and re-layouts  11.3 us (3%)
  other arithmetic  8.15 us (2%)
    reduce_scatter x1, waiting for transfers between devices, local(): lax.psum_scatter(jnp.dot(columns_all, out_weight, preferred_element_type=...  218 us
    all_to_all x1, blocking collectives, local(): lax.all_to_all(attended, 'fsdp', split_axis=1, concat_axis=0, tiled=True)  35.4 us
    all_to_all x1, blocking collectives, local(): lax.all_to_all(head_rows, 'cam', split_axis=0, concat_axis=1, tiled=True)  20.6 us
    all_to_all x1, waiting for transfers between devices, local(): lax.all_to_all(query_rows, 'cam', split_axis=1, concat_axis=0, tiled=True)  16.2 us
    all_to_all x1, waiting for transfers between devices, local(): lax.all_to_all(keys[0], 'cam', split_axis=1, concat_axis=0, tiled=True)  14.7 us
    dot_general x1, matrix products, local(): jnp.dot(columns_all, out_weight, preferred_element_type=jnp.float32)  13.8 us
    dot_general x4, matrix products, one_block(): jnp.einsum('qd,kd->qk', query_block, key_h, preferred_element_type=jnp.fl...  13.7 us
    dot_general x4, matrix products, one_block(): jnp.dot(weights, value_h, preferred_element_type=jnp.float32)  11.5 us
  transfers between devices with their start and end apart: 5, of which 5 were waited for; matrix products, arithmetic and copies ran while one was open for 6% of the time, Pallas kernels for 0%

commit v1 on v0

--- a/solution.py
+++ b/solution.py
@@ -41,29 +41,25 @@
 
 
 def local(queries, keys, values, out_weight, block_counts, row_mask):
-    query_rows = queries[0]
-    row_count = query_rows.shape[0]
+    row_count = queries.shape[1]
     cam_count = lax.axis_size("cam")
+    place = lax.axis_index("cam")
+    columns = out_weight.shape[1] // cam_count
     offsets = jnp.arange(row_count, dtype=jnp.int32)
     row_valid = (row_mask[0] == 1) & (offsets // BLOCK < block_counts[0, 0])
-    key_flag = jnp.broadcast_to(row_valid.astype(jnp.bfloat16)[:, None], (row_count, cam_count))
-    query_all, key_all, value_all, flag_all = (
-        lax.all_to_all(query_rows, "cam", split_axis=1, concat_axis=0, tiled=True),
-        lax.all_to_all(keys[0], "cam", split_axis=1, concat_axis=0, tiled=True),
-        lax.all_to_all(values[0], "cam", split_axis=1, concat_axis=0, tiled=True),
-        lax.all_to_all(key_flag, "cam", split_axis=1, concat_axis=0, tiled=True),
+    weight_part = lax.dynamic_slice_in_dim(out_weight, place * columns, columns, axis=1)
+    weight_all = lax.all_gather(weight_part, "fsdp", axis=0, tiled=True)
+
+    key_flag = lax.all_gather(row_valid.astype(jnp.bfloat16), "cam", axis=0, tiled=True)
+    stacked = jnp.concatenate([queries, keys, values], axis=0)
+    exchanged = lax.all_to_all(stacked, "cam", split_axis=2, concat_axis=1, tiled=True)
+    head_rows = attend(exchanged[0], exchanged[1], exchanged[2], key_flag > 0.5)
+    attended = lax.all_gather(head_rows, "cam", axis=1, tiled=True)
+    projected = jnp.dot(attended, weight_all, preferred_element_type=jnp.float32).astype(
+        jnp.bfloat16
     )
-    head_rows = attend(query_all, key_all, value_all, flag_all[:, 0] > 0.5)
-    attended = lax.all_to_all(head_rows, "cam", split_axis=0, concat_axis=1, tiled=True)
-    columns_all = lax.all_to_all(attended, "fsdp", split_axis=1, concat_axis=0, tiled=True)
-    projected = lax.psum_scatter(
-        jnp.dot(columns_all, out_weight, preferred_element_type=jnp.float32),
-        "fsdp",
-        scatter_dimension=0,
-        tiled=True,
-    )
-    result = jnp.where(row_valid[:, None], projected, jnp.float32(0.0)).astype(jnp.bfloat16)
-    return result[None]
+    result = lax.all_to_all(projected, "cam", split_axis=0, concat_axis=1, tiled=True)
+    return jnp.where(row_valid[:, None], result, jnp.bfloat16(0.0))[None]
 
 
 def solution(mesh):

time: 400 us -> 255 us (0.64)
  waiting for transfers between devices: 254 us -> 72.4 us
  local copies, waits for them, and re-layouts: 11.3 us -> 55.8 us
  blocking collectives: 56 us -> 72.9 us
  matrix products: 39.1 us -> 22.5 us
  starting transfers between devices: 16.6 us -> 5.25 us
    reduce_scatter x1 -> x0, waiting for transfers between devices: 218 us -> none  [local(): lax.psum_scatter(jnp.dot(columns_all, out_weight, preferred_element_type=...]
    all_gather x0 -> x2, waiting for transfers between devices: none -> 72.4 us  [the longest x1 63.6 us: local(): attended = lax.all_gather(head_rows, 'cam', axis=1, tiled=True)]
    unnamed x0 -> x1, blocking collectives: none -> 48.6 us
    all_to_all x4 -> x1, waiting for transfers between devices: 35.7 us -> 0.01 us  [local(): lax.all_to_all(stacked, 'cam', split_axis=2, concat_axis=1, tiled=True)]
    all_to_all x2 -> x1, blocking collectives: 56 us -> 24.2 us  [local(): lax.all_to_all(projected, 'cam', split_axis=0, concat_axis=1, tiled=True)]
    unnamed x23 -> x9, local copies, waits for them, and re-layouts: 4.21 us -> 26.1 us
    concatenate x0 -> x1, local copies, waits for them, and re-layouts: none -> 12.6 us  [local(): stacked = jnp.concatenate([queries, keys, values], axis=0)]
    all_to_all x4 -> x1, starting transfers between devices: 16.6 us -> 5.17 us  [local(): lax.all_to_all(stacked, 'cam', split_axis=2, concat_axis=1, tiled=True)]
  transfers between devices with their start and end apart: 5 -> 3, of which waited for: 5 -> 2; matrix products, arithmetic and copies ran while one was open for 6% -> 17% of each run, Pallas kernels for 0% -> 0%
where the time goes in v1:
time: 255 us; the launch traced here: 254 us
  blocking collectives  72.9 us (29%)
  waiting for transfers between devices  72.4 us (28%)
  local copies, waits for them, and re-layouts  55.8 us (22%)
  matrix products  22.5 us (9%)
  between operations  14.9 us (6%)
  other arithmetic  10 us (4%)
  starting transfers between devices  5.25 us (2%)
    all_gather x1, waiting for transfers between devices, local(): attended = lax.all_gather(head_rows, 'cam', axis=1, tiled=True)  63.6 us
    unnamed x1, blocking collectives  48.6 us
    unnamed x9, local copies, waits for them, and re-layouts  26.1 us
    all_to_all x1, blocking collectives, local(): lax.all_to_all(projected, 'cam', split_axis=0, concat_axis=1, tiled=True)  24.2 us
    concatenate x1, local copies, waits for them, and re-layouts, local(): stacked = jnp.concatenate([queries, keys, values], axis=0)  12.6 us
    dot_general x1, matrix products, local(): jnp.dot(attended, weight_all, preferred_element_type=jnp.float32)  12.6 us
    all_to_all x1, local copies, waits for them, and re-layouts, local(): lax.all_to_all(stacked, 'cam', split_axis=2, concat_axis=1, tiled=True)  9.55 us
    all_gather x1, waiting for transfers between devices, local(): weight_all = lax.all_gather(weight_part, 'fsdp', axis=0, tiled=True)  8.84 us
  transfers between devices with their start and end apart: 3, of which 2 were waited for; matrix products, arithmetic and copies ran while one was open for 17% of the time, Pallas kernels for 0%

profile of v1, /device:TPU:0, one launch (start us, length us, event | category | flops | bytes accessed | tf_op | source)
XLA Modules:
  0.0 253.7 jit_solution(16722625092312821470)
XLA Ops:
  6.5 3.6 %pad_maximum_fusion = bf16[3,160,4096]{2,1,0:T(8,128)(2,1)} fusion(bf16[1,160,4096]{2,1,0:T(8,128)(2,1)} %param.8, bf16[1,160,4096]{2,1,0:T(8,128)(2,1)} %param.7, bf16[1,160,4096]{2,1,0:T(8,128)(2,1)} %param.6), kind=kLoop, calls=%fused_computation.20 | loop fusion | flops 3932160 | bytes 7864320 | tf_op jit(solution)/shard_map/concatenate | solution.py:54
  10.1 12.6 %copy.21 = bf16[3,160,4096]{1,0,2:T(4,128)(2,1)} copy(bf16[3,160,4096]{2,1,0:T(8,128)(2,1)} %pad_maximum_fusion) | data formatting | bytes 7864320 | tf_op jit(solution)/shard_map/concatenate | solution.py:54
  22.8 12.5 %reshape.95 = bf16[8,2,122880]{2,1,0:T(2,128)(2,1)} reshape(bf16[4096,3,160]{2,1,0:T(4,128)(2,1)} %bitcast.14) | data formatting | bytes 7864320
  35.3 5.2 %all-to-all-start = ((bf16[8,2,122880]{2,1,0:T(2,128)(2,1)}), bf16[8,2,122880]{2,1,0:T(2,128)(2,1)}, u32[]{:S(2)}, u32[]{:S(2)}) async-start(bf16[8,2,122880]{2,1,0:T(2,128)(2,1)} %reshape.95), calls=%async_computation | async-start | bytes 7864320 | tf_op jit(solution)/shard_map/all_to_all | solution.py:55
  40.5 0.0 copy-start.1
  40.5 0.0 copy-start
  40.5 0.0 all-gather.5.cloned.1.call-start
  40.5 2.5 constant_dynamic-slice_fusion
  43.1 0.0 all-gather.5.cloned.1.call-update
  43.1 0.0 all-gather.3.cloned.1.call-start
  43.8 0.0 copy-done.1
  43.8 0.6 dynamic-slice.4
  45.1 0.0 copy-done
  45.2 0.2 dynamic-update-slice
  45.4 48.6 %all-reduce = bf16[1280]{0:T(1024)(128)(2,1)S(1)} all-reduce(bf16[1280]{0:T(1024)(128)(2,1)S(1)} %dynamic-update-slice), channel_id=1, replica_groups=mesh['cam'=8,'fsdp'=4] {'cam'}, use_global_device_ids=true, to_apply=%add | all-reduce | flops 1280 | bytes 5120
  94.1 0.0 all-to-all-done
  94.1 12.7 %reshape.96 = bf16[4096,3,160]{2,1,0:T(4,128)(2,1)} reshape(bf16[8,2,122880]{2,1,0:T(2,128)(2,1)} %all-to-all-done) | data formatting | bytes 7864320
  106.8 9.6 %copy.27 = bf16[3,160,8,512]{3,2,1,0:T(8,128)(2,1)} copy(bf16[3,160,8,512]{1,0,3,2:T(4,128)(2,1)} %bitcast.15) | data formatting | bytes 7864320 | tf_op jit(solution)/shard_map/all_to_all | solution.py:55
  116.3 2.4 fusion.29
  118.7 0.4 copy.23
  119.1 0.4 copy.24
  119.5 0.4 copy.25
  120.0 1.1 fusion.33
  121.1 1.0 fusion.4
  122.0 1.1 fusion.32
  123.1 1.0 fusion.5
  124.1 1.1 fusion.31
  125.2 1.0 fusion.6
  126.2 1.1 fusion.30
  127.3 1.0 fusion.7
  128.3 1.3 fusion.15
  129.6 1.5 fusion.14
  131.1 1.3 fusion.13
  132.4 1.3 fusion.12
  133.7 1.1 pad_maximum_fusion.1
  134.9 0.0 all-gather.3.cloned.1.call-update
  134.9 8.8 %all-gather.5.cloned.1.call-done = bf16[4096,640]{1,0:T(8,128)(2,1)} async-done(((bf16[1024,640]{1,0:T(8,128)(2,1)}), bf16[4096,640]{1,0:T(8,128)(2,1)}) %all-gather.5.cloned.1.call-update) | async-done | bytes 5242896 | tf_op jit(solution)/shard_map/all_gather | solution.py:51
  143.7 63.6 %all-gather.3.cloned.1.call-done = bf16[1280,4096]{0,1:T(8,128)(2,1)} async-done(((bf16[1280,512]{0,1:T(8,128)(2,1)}), bf16[1280,4096]{0,1:T(8,128)(2,1)}) %all-gather.3.cloned.1.call-update) | async-done | bytes 10485776 | tf_op jit(solution)/shard_map/all_gather | solution.py:57
  207.3 12.6 %convolution_convert_fusion = bf16[1280,640]{1,0:T(8,128)(2,1)S(1)} fusion(bf16[1280,4096]{0,1:T(8,128)(2,1)} %all-gather.3.cloned.1.call-done, bf16[4096,640]{1,0:T(8,128)(2,1)} %all-gather.5.cloned.1.call-done), kind=kOutput, calls=%fused_computation.25 | convolution fusion | flops 6711705600 | bytes 17367040 | tf_op jit(solution)/shard_map/dot_general | solution.py:58
  219.9 24.2 %all_to_all.34 = bf16[8,160,640]{2,1,0:T(8,128)(2,1)S(1)} all-to-all(bf16[8,160,640]{2,1,0:T(8,128)(2,1)S(1)} %bitcast.26), channel_id=1, replica_groups=mesh['cam'=8,'fsdp'=4] {'cam'}, dimensions={0} | all-to-all | bytes 3276800 | tf_op jit(solution)/shard_map/all_to_all | solution.py:61
  244.2 0.5 copy.26
  244.7 0.8 all_to_all.31
  245.5 1.3 broadcast_select_fusion
  (4 shorter events, 0.0 us)
Async XLA Ops:
  35.3 58.8 %all-to-all-start = ((bf16[8,2,122880]{2,1,0:T(2,128)(2,1)}), bf16[8,2,122880]{2,1,0:T(2,128)(2,1)}, u32[]{:S(2)}, u32[]{:S(2)}) async-start(bf16[8,2,122880]{2,1,0:T(2,128)(2,1)} %reshape.95), calls=%async_computation | async-start | bytes 7864320 | tf_op jit(solution)/shard_map/all_to_all | solution.py:55
  40.5 3.3 %copy-start.1 = (u32[32]{0:T(128)S(1)}, u32[32]{0:T(128)}, u32[]{:S(2)}) copy-start(u32[32]{0:T(128)} %constant.106) | copy-start | bytes 388
  40.5 4.7 %copy-start = (s32[1,160]{1,0:T(1,128)S(1)}, s32[1,160]{1,0:T(1,128)}, u32[]{:S(2)}) copy-start(s32[1,160]{1,0:T(1,128)} %param.11) | copy-start | bytes 1924
  40.5 103.3 %all-gather.5.cloned.1.call-start = ((), (), s32[]{:S(2)}) async-start(), calls=%async_computation.3 | async-start | bytes 6553600 | tf_op jit(solution)/shard_map/all_gather | solution.py:51
  43.1 164.2 %all-gather.3.cloned.1.call-start = ((), (), s32[]{:S(2)}) async-start(), calls=%async_computation.2 | async-start | bytes 11796480 | tf_op jit(solution)/shard_map/all_gather | solution.py:57
Sparse Core Ops, SparseCore 0:
  43.2 100.4 all-gather.4
  145.6 61.6 all-gather.2

commit v2 on v1

v2 whole, which is shorter than its diff:
```python
import math

import jax
import jax.numpy as jnp
from jax import lax
from jax.experimental import pallas as pl
from jax.experimental.pallas import tpu as pltpu
from jax.sharding import PartitionSpec as P

HEAD_DIM = 128
BLOCK = 32
SENTINEL = 32.0
LIMIT = 24.0
VMEM = 56 * 1024 * 1024
QUERY_TILE = 256


def params(limit=VMEM):
    return pltpu.CompilerParams(vmem_limit_bytes=limit)


def xor_permute(array, mask, count):
    return lax.ppermute(array, "cam", [(place, place ^ mask) for place in range(count)])


def pack(place, queries, keys, values, valid_column, count):
    rows, features = queries.shape
    width = features // count
    step = BLOCK

    def body(place_ref, q_ref, k_ref, v_ref, valid_ref, *out_refs):
        good = valid_ref[...] > 0.5
        for mask in range(count):
            start = pl.multiple_of((place_ref[0] ^ mask) * width, HEAD_DIM)
            chosen = pl.ds(start, width)
            out_refs[mask][0] = q_ref[:, chosen]
            out_refs[mask][1] = jnp.where(good, k_ref[:, chosen], jnp.bfloat16(SENTINEL))
            out_refs[mask][2] = v_ref[:, chosen]

    row_spec = pl.BlockSpec((step, features), lambda i, place_ref: (i, 0))
    return pl.pallas_call(
        body,
        grid_spec=pltpu.PrefetchScalarGridSpec(
            num_scalar_prefetch=1,
            grid=(rows // step,),
            in_specs=[row_spec, row_spec, row_spec]
            + [pl.BlockSpec((step, 1), lambda i, place_ref: (i, 0))],
            out_specs=[pl.BlockSpec((3, step, width), lambda i, place_ref: (0, i, 0))] * count,
        ),
        out_shape=[jax.ShapeDtypeStruct((3, rows, width), jnp.bfloat16)] * count,
        compiler_params=params(),
        cost_estimate=pl.CostEstimate(
            flops=0, bytes_accessed=12 * rows * features, transcendentals=0
        ),
        name="pack",
    )(place, queries, keys, values, valid_column)


def attend(place, received, rows):
    count = len(received)
    width = received[0].shape[2]
    total = count * rows
    factor = math.log2(math.e) / math.sqrt(HEAD_DIM)

    def body(place_ref, *refs):
        parts = refs[:count]
        out_ref = refs[count]
        query_all, key_all, value_t, result = refs[count + 1 :]
        for mask in range(count):
            where = pl.ds(mask * rows, rows)
            query_all[where, :] = parts[mask][0]
            key_all[where, :] = parts[mask][1]
        value_all = jnp.concatenate([parts[mask][2] for mask in range(count)], axis=0)
        value_t[...] = value_all.T
        key_rows = key_all[...]
        bias = jnp.where(key_rows.astype(jnp.float32) > LIMIT, jnp.float32(-1e30), 0.0)
        bias = jnp.concatenate([bias] * (QUERY_TILE // HEAD_DIM), axis=1)
        for tile in range(total // QUERY_TILE):
            where = pl.ds(tile * QUERY_TILE, QUERY_TILE)
            scores = lax.dot_general(
                key_rows,
                query_all[where, :],
                (((1,), (1,)), ((), ())),
                preferred_element_type=jnp.float32,
            )
            scores = scores + bias
            top = jnp.max(scores, axis=0, keepdims=True)
            raised = jnp.exp2((scores - top) * factor)
            norm = jnp.sum(raised, axis=0, keepdims=True)
            summed = jnp.dot(
                value_t[...], raised.astype(jnp.bfloat16), preferred_element_type=jnp.float32
            )
            result[where, :] = (summed / norm).T.astype(jnp.bfloat16)
        for mask in range(count):
            out_ref[pl.ds(place_ref[0] ^ mask, 1)] = result[pl.ds(mask * rows, rows), :][None]

    flops = 4 * total * total * width
    return pl.pallas_call(
        body,
        grid_spec=pltpu.PrefetchScalarGridSpec(
            num_scalar_prefetch=1,
            grid=(width // HEAD_DIM,),
            in_specs=[pl.BlockSpec((3, rows, HEAD_DIM), lambda h, place_ref: (0, 0, h))] * count,
            out_specs=pl.BlockSpec((count, rows, HEAD_DIM), lambda h, place_ref: (0, 0, h)),
            scratch_shapes=[
                pltpu.VMEM((total, HEAD_DIM), jnp.bfloat16),
                pltpu.VMEM((total, HEAD_DIM), jnp.bfloat16),
                pltpu.VMEM((HEAD_DIM, total), jnp.bfloat16),
                pltpu.VMEM((total, HEAD_DIM), jnp.bfloat16),
            ],
        ),
        out_shape=jax.ShapeDtypeStruct((count, rows, width), jnp.bfloat16),
        compiler_params=params(),
        cost_estimate=pl.CostEstimate(
            flops=flops, bytes_accessed=8 * total * width, transcendentals=flops // 512
        ),
        name="attend",
    )(place, *received)


def gather_features(own, count):
    half = count // 2
    held = {0: [own[:half], own[half:]]}
    if count == 8:
        over_x_0 = xor_permute(held[0][0], 2, count)
        over_y_1 = xor_permute(held[0][1], 4, count)
        over_x_1 = xor_permute(held[0][1], 2, count)
        over_y_0 = xor_permute(held[0][0], 4, count)
        diagonal_0 = xor_permute(over_x_0, 4, count)
        diagonal_1 = xor_permute(over_y_1, 2, count)
        held[2] = [over_x_0, over_x_1]
        held[4] = [over_y_0, over_y_1]
        held[6] = [diagonal_0, diagonal_1]
    else:
        for mask in range(2, count, 2):
            held[mask] = [xor_permute(piece, mask, count) for piece in held[0]]
    for mask in range(0, count, 2):
        held[mask + 1] = [xor_permute(piece, 1, count) for piece in held[mask]]
    return [held[mask] for mask in range(count)]


def project(place, features, weight):
    count = len(features)
    half, rows, width = features[0][0].shape
    columns = weight.shape[1]

    def body(place_ref, *refs):
        halves = refs[: 2 * count]
        weight_ref = refs[2 * count]
        out_refs = refs[2 * count + 1 : 3 * count + 1]
        landed, weight_all, total, sems, weight_sems = refs[3 * count + 1 :]
        copies = []
        weight_copies = []
        for mask in range(count):
            start = pl.multiple_of((place_ref[0] ^ mask) * width, width)
            copy = pltpu.make_async_copy(
                weight_ref.at[pl.ds(start, width), :], weight_all.at[mask], weight_sems.at[mask]
            )
            copy.start()
            weight_copies.append(copy)
            for side in range(2):
                copy = pltpu.make_async_copy(
                    halves[2 * mask + side], landed.at[mask, side], sems.at[mask, side]
                )
                copy.start()
                copies.append(copy)
        for mask in range(count):
            weight_copies[mask].wait()
            for side in range(2):
                copies[2 * mask + side].wait()
                part = jnp.dot(
                    landed[mask, side].reshape(half * rows, width),
                    weight_all[mask],
                    preferred_element_type=jnp.float32,
                )
                if mask == 0:
                    total[side] = part.reshape(half, rows, columns)
                else:
                    total[side] += part.reshape(half, rows, columns)
        for mask in range(count):
            view = place_ref[0] ^ mask
            out_refs[mask][...] = total[view // half, view % half].astype(jnp.bfloat16)

    any_spec = pl.BlockSpec(memory_space=pl.ANY)
    flat = [piece for pair in features for piece in pair]
    return pl.pallas_call(
        body,
        grid_spec=pltpu.PrefetchScalarGridSpec(
            num_scalar_prefetch=1,
            grid=(1,),
            in_specs=[any_spec] * (2 * count + 1),
            out_specs=[pl.BlockSpec((rows, columns), lambda i, place_ref: (0, 0))] * count,
            scratch_shapes=[
                pltpu.VMEM((count, 2, half, rows, width), jnp.bfloat16),
                pltpu.VMEM((count, width, columns), jnp.bfloat16),
                pltpu.VMEM((2, half, rows, columns), jnp.float32),
                pltpu.SemaphoreType.DMA((count, 2)),
                pltpu.SemaphoreType.DMA((count,)),
            ],
        ),
        out_shape=[jax.ShapeDtypeStruct((rows, columns), jnp.bfloat16)] * count,
        compiler_params=params(),
        cost_estimate=pl.CostEstimate(
            flops=2 * count * rows * count * width * columns,
            bytes_accessed=2 * count * count * rows * width,
            transcendentals=0,
        ),
        name="project",
    )(place, *flat, weight)


def assemble(place, chunks, sizes, valid_column, count):
    rows = valid_column.shape[0]
    columns = sum(sizes)
    if any(size % HEAD_DIM for size in sizes):
        joined = [
            jnp.concatenate([chunk[mask] for chunk in chunks], axis=1) for mask in range(count)
        ]
        stacked = jnp.stack(joined)[jnp.arange(count) ^ place[0]]
        result = jnp.moveaxis(stacked, 0, 1).reshape(rows, count * columns)
        return jnp.where(valid_column > 0.5, result, jnp.bfloat16(0.0))

    def body(place_ref, valid_ref, *refs):
        out_ref = refs[-1]
        good = valid_ref[...] > 0.5
        for index in range(len(sizes)):
            for mask in range(count):
                start = (place_ref[0] ^ mask) * columns + sum(sizes[:index])
                chosen = pl.ds(pl.multiple_of(start, HEAD_DIM), sizes[index])
                piece = refs[index * count + mask][...]
                out_ref[:, chosen] = jnp.where(good, piece, jnp.bfloat16(0.0))

    step = BLOCK
    return pl.pallas_call(
        body,
        grid_spec=pltpu.PrefetchScalarGridSpec(
            num_scalar_prefetch=1,
            grid=(rows // step,),
            in_specs=[pl.BlockSpec((step, 1), lambda i, place_ref: (i, 0))]
            + [
                pl.BlockSpec((step, size), lambda i, place_ref: (i, 0))
                for size in sizes
                for mask in range(count)
            ],
            out_specs=pl.BlockSpec((step, count * columns), lambda i, place_ref: (i, 0)),
        ),
        out_shape=jax.ShapeDtypeStruct((rows, count * columns), jnp.bfloat16),
        compiler_params=params(),
        cost_estimate=pl.CostEstimate(
            flops=0, bytes_accessed=4 * rows * count * columns, transcendentals=0
        ),
        name="assemble",
    )(place, valid_column, *[piece for chunk in chunks for piece in chunk])


def local(queries, keys, values, out_weight, block_counts, row_mask):
    rows = queries.shape[1]
    count = lax.axis_size("cam")
    place = lax.axis_index("cam")
    place_array = jnp.full((1,), place, jnp.int32)
    columns = out_weight.shape[1] // count
    first = max(HEAD_DIM, -(-columns * 3 // 5 // HEAD_DIM) * HEAD_DIM)
    sizes = [first, columns - first]

    offsets = jnp.arange(rows, dtype=jnp.int32)
    row_valid = (row_mask[0] == 1) & (offsets // BLOCK < block_counts[0, 0])
    valid_column = row_valid.astype(jnp.float32)[:, None]

    weights = []
    for index, size in enumerate(sizes):
        start = place * columns + sum(sizes[:index])
        part = lax.dynamic_slice_in_dim(out_weight, start, size, axis=1)
        weights.append(part)
    weights[0], weights[1], queries = lax.optimization_barrier((weights[0], weights[1], queries))
    weights = [lax.all_gather(part, "fsdp", axis=0, tiled=True) for part in weights]

    payloads = pack(place_array, queries[0], keys[0], values[0], valid_column, count)
    received = [payloads[0]] + [
        xor_permute(payloads[mask], mask, count) for mask in range(1, count)
    ]
    attended = attend(place_array, received, rows)
    features = gather_features(attended, count)
    chunks = []
    for weight in weights:
        pieces = project(place_array, features, weight)
        chunks.append(
            [pieces[0]] + [xor_permute(pieces[mask], mask, count) for mask in range(1, count)]
        )
    return assemble(place_array, chunks, sizes, valid_column, count)[None]


def solution(mesh):
    in_specs = (
        P("fsdp", "cam", None),
        P("fsdp", "cam", None),
        P("fsdp", "cam", None),
        P("fsdp", None),
        P("fsdp", "cam"),
        P("fsdp", "cam"),
    )
    out_specs = P("fsdp", "cam", None)
    return jax.shard_map(local, mesh=mesh, in_specs=in_specs, out_specs=out_specs, check_vma=False)
```

time: 255 us -> 200 us (0.78)
  blocking collectives: 72.9 us -> 0 us
  Pallas kernels: 0 us -> 50.9 us
  local copies, waits for them, and re-layouts: 55.8 us -> 8.29 us
  starting transfers between devices: 5.25 us -> 34.5 us
  matrix products: 22.5 us -> 0 us
  waiting for transfers between devices: 72.4 us -> 90.4 us
  other arithmetic: 10 us -> 0.66 us
    ppermute x0 -> x35, waiting for transfers between devices: none -> 89.7 us  [xor_permute(): lax.ppermute(array, 'cam', [(place, place ^ mask) for place in range(coun...]
    all_gather x2, waiting for transfers between devices: 72.4 us -> 0.01 us  [local(): lax.all_gather(part, 'fsdp', axis=0, tiled=True)]
    pallas_call x0 -> x5, Pallas kernels: none -> 50.9 us  [the longest x2 21.7 us: project(): pl.pallas_call(body, grid_spec=pltpu.PrefetchScalarGridSpec(num_scalar_pr...]
    unnamed x1 -> x0, blocking collectives: 48.6 us -> none
    ppermute x0 -> x35, starting transfers between devices: none -> 34.5 us  [xor_permute(): lax.ppermute(array, 'cam', [(place, place ^ mask) for place in range(coun...]
    all_to_all x1 -> x0, blocking collectives: 24.2 us -> none  [local(): lax.all_to_all(projected, 'cam', split_axis=0, concat_axis=1, tiled=True)]
    unnamed x9 -> x80, local copies, waits for them, and re-layouts: 26.1 us -> 2.7 us
    dot_general x9 -> x0, matrix products: 22.5 us -> none  [the longest x1 12.6 us: local(): jnp.dot(attended, weight_all, preferred_element_type=jnp.float32)]
  transfers between devices with their start and end apart: 3 -> 37, of which waited for: 2 -> 12; matrix products, arithmetic and copies ran while one was open for 17% -> 1% of each run, Pallas kernels for 0% -> 23%
where the time goes in v2:
time: 200 us; the launch traced here: 199 us
  waiting for transfers between devices  90.4 us (45%)
  Pallas kernels  50.9 us (25%)
  starting transfers between devices  34.5 us (17%)
  between operations  14.5 us (7%)
  local copies, waits for them, and re-layouts  8.29 us (4%)
    ppermute x35, waiting for transfers between devices, xor_permute(): lax.ppermute(array, 'cam', [(place, place ^ mask) for place in range(coun...  89.7 us
    ppermute x35, starting transfers between devices, xor_permute(): lax.ppermute(array, 'cam', [(place, place ^ mask) for place in range(coun...  34.5 us
    pallas_call x2, Pallas kernels, project(): pl.pallas_call(body, grid_spec=pltpu.PrefetchScalarGridSpec(num_scalar_pr...  21.7 us
    pallas_call x1, Pallas kernels, attend(): pl.pallas_call(body, grid_spec=pltpu.PrefetchScalarGridSpec(num_scalar_pr...  19.4 us
    pallas_call x1, Pallas kernels, pack(): pl.pallas_call(body, grid_spec=pltpu.PrefetchScalarGridSpec(num_scalar_pr...  5.7 us
    pallas_call x1, Pallas kernels, assemble(): pl.pallas_call(body, grid_spec=pltpu.PrefetchScalarGridSpec(num_scalar_pr...  4.2 us
    dynamic_slice x2, local copies, waits for them, and re-layouts, local(): part = lax.dynamic_slice_in_dim(out_weight, start, size, axis=1)  4.02 us
  transfers between devices with their start and end apart: 37, of which 12 were waited for; matrix products, arithmetic and copies ran while one was open for 1% of the time, Pallas kernels for 23%

profile of v2, /device:TPU:0, one launch (start us, length us, event | category | flops | bytes accessed | tf_op | source)
XLA Modules:
  0.0 199.3 jit_solution(9480713586158412353)
XLA Ops:
  6.5 2.1 %constant_dynamic-slice_fusion.1 = bf16[1024,384]{1,0:T(8,128)(2,1)} fusion(bf16[1024,5120]{1,0:T(8,128)(2,1)} %param.9, s32[]{:T(128)S(6)} %select_n.19), kind=kLoop, calls=%fused_computation.12 | loop fusion | bytes 1572868 | tf_op jit(solution)/shard_map/dynamic_slice | solution.py:272
  8.7 1.9 constant_dynamic-slice_fusion
  10.6 0.7 all-gather.3.cloned.1.call-update
  12.2 0.7 fusion.5.valid_ref
  12.8 5.7 %pack.1 = (bf16[3,160,512]{2,1,0:T(8,128)(2,1)}, bf16[3,160,512]{2,1,0:T(8,128)(2,1)}, bf16[3,160,512]{2,1,0:T(8,128)(2,1)}, bf16[3,160,512]{2,1,0:T(8,128)(2,1)...) custom-call(s32[1]{0:T(128)} %bitcast.place_ref, ...), custom_call_target="tpu_custom_call" | custom-call | bytes 7864320 | tf_op jit(solution)/shard_map/pack/pallas_call | solution.py:41
  18.5 0.5 collective-permute-start
  19.0 2.6 %collective-permute-start.1 = (bf16[3,160,512]{2,1,0:T(8,128)(2,1)}, bf16[3,160,512]{2,1,0:T(8,128)(2,1)S(1)}, u32[]{:S(2)}, u32[]{:S(2)}) collective-permute-start(bf16[3,160,512]{2,1,0:T(8,128)(2,1)} %get-tuple-element.35), channel_id=1, source_target_pairs={{0,8},{4,12},{8,0},{12,4},{16,24},{20,28},{24,16},{28,20},{1,9},{5... | collective-permute-start | bytes 1474568 | tf_op jit(solution)/shard_map/ppermute | solution.py:23
  21.7 1.8 collective-permute-start.3
  23.4 2.6 %collective-permute-start.5 = (bf16[3,160,512]{2,1,0:T(8,128)(2,1)}, bf16[3,160,512]{2,1,0:T(8,128)(2,1)S(1)}, u32[]{:S(2)}, u32[]{:S(2)}) collective-permute-start(bf16[3,160,512]{2,1,0:T(8,128)(2,1)} %get-tuple-element.39), channel_id=1, source_target_pairs={{0,24},{4,28},{8,16},{12,20},{16,8},{20,12},{24,0},{28,4},{1,25},{... | collective-permute-start | bytes 1474568 | tf_op jit(solution)/shard_map/ppermute | solution.py:23
  26.0 7.8 %collective-permute-done.1.refs_2_ = bf16[3,160,512]{2,1,0:T(8,128)(2,1)S(1)} collective-permute-done((bf16[3,160,512]{2,1,0:T(8,128)(2,1)}, bf16[3,160,512]{2,1,0:T(8,128)(2,1)S(1)}, u32[]{:S(2)}, u32[]{:S(2)}) %collective-permute-start.1) | collective-permute-done | bytes 491552 | tf_op jit(solution)/shard_map/ppermute | solution.py:23
  33.9 1.8 collective-permute-start.6
  35.7 8.3 %collective-permute-done.2.refs_3_ = bf16[3,160,512]{2,1,0:T(8,128)(2,1)S(1)} collective-permute-done((bf16[3,160,512]{2,1,0:T(8,128)(2,1)}, bf16[3,160,512]{2,1,0:T(8,128)(2,1)S(1)}, u32[]{:S(2)}, u32[]{:S(2)}) %collective-permute-start.2) | collective-permute-done | bytes 491552 | tf_op jit(solution)/shard_map/ppermute | solution.py:23
  44.0 22.3 %collective-permute-done.4.refs_5_ = bf16[3,160,512]{2,1,0:T(8,128)(2,1)S(1)} collective-permute-done((bf16[3,160,512]{2,1,0:T(8,128)(2,1)}, bf16[3,160,512]{2,1,0:T(8,128)(2,1)S(1)}, u32[]{:S(2)}, u32[]{:S(2)}) %collective-permute-start.4) | collective-permute-done | bytes 491552 | tf_op jit(solution)/shard_map/ppermute | solution.py:23
  66.4 0.8 copy-done.34
  67.3 0.2 copy-done.36
  67.5 19.4 %attend.1 = bf16[8,160,512]{2,1,0:T(8,128)(2,1)} custom-call(s32[1]{0:T(128)} %bitcast.place_ref, bf16[3,160,512]{2,1,0:T(8,128)(2,1)} %get-tuple-element.33.refs_0_, bf16[3,160,512]{2,1,0:T(8,128)(2,1)} %copy-done.30, bf16[3,160,512]{2,1,0:T(8,128)(2,1)} %copy-done.31, bf16[3,160,512]{2,1,0:T(8,128)(2,1)} %copy-done.32, bf16[3,160,512]{2,1,0:T(8,128)(2,1)} %copy-done.33, ...), custom_call_target="tpu_custom_call" | custom-call | flops 3355443200 | bytes 5242880 | tf_op jit(solution)/shard_map/attend/pallas_call | solution.py:98
  86.9 1.4 fusion.6
  88.3 0.5 collective-permute-start.7
  88.8 1.7 collective-permute-start.9
  90.5 1.5 collective-permute-start.14
  92.1 0.5 collective-permute-start.10
  92.6 0.3 collective-permute-start.13
  92.9 13.5 %collective-permute-done.9.refs_4_ = bf16[4,160,512]{2,1,0:T(8,128)(2,1)S(1)} collective-permute-done((bf16[4,160,512]{2,1,0:T(8,128)(2,1)S(1)}, bf16[4,160,512]{2,1,0:T(8,128)(2,1)S(1)}, u32[]{:S(2)}, u32[]{:S(2)}) %collective-permute-start.9) | collective-permute-done | bytes 655392 | tf_op jit(solution)/shard_map/ppermute | solution.py:23
  106.4 1.8 collective-permute-start.17
  108.3 1.5 collective-permute-start.18
  109.7 10.7 %collective-permute-done.10.refs_5_ = bf16[4,160,512]{2,1,0:T(8,128)(2,1)S(1)} collective-permute-done((bf16[4,160,512]{2,1,0:T(8,128)(2,1)S(1)}, bf16[4,160,512]{2,1,0:T(8,128)(2,1)S(1)}, u32[]{:S(2)}, u32[]{:S(2)}) %collective-permute-start.10) | collective-permute-done | bytes 655392 | tf_op jit(solution)/shard_map/ppermute | solution.py:23
  120.5 1.7 collective-permute-done.13.refs_8_
  122.1 0.5 collective-permute-start.15
  122.6 13.1 %collective-permute-done.17.refs_12_ = bf16[4,160,512]{2,1,0:T(8,128)(2,1)S(1)} collective-permute-done((bf16[4,160,512]{2,1,0:T(8,128)(2,1)S(1)}, bf16[4,160,512]{2,1,0:T(8,128)(2,1)S(1)}, u32[]{:S(2)}, u32[]{:S(2)}) %collective-permute-start.17) | collective-permute-done | bytes 655392 | tf_op jit(solution)/shard_map/ppermute | solution.py:23
  135.8 0.5 collective-permute-start.20
  136.4 1.6 collective-permute-done.19.refs_14_
  138.0 0.8 copy-done.14
  139.0 9.8 %project.3 = (bf16[160,256]{1,0:T(8,128)(2,1)}, bf16[160,256]{1,0:T(8,128)(2,1)}, bf16[160,256]{1,0:T(8,128)(2,1)}, bf16[160,256]{1,0:T(8,128)(2,1)}, bf16[160,2...) custom-call(s32[1]{0:T(128)} %bitcast.place_ref, ...), custom_call_target="tpu_custom_call" | custom-call | flops 2684354560 | bytes 10485760 | tf_op jit(solution)/shard_map/project/pallas_call | solution.py:186
  149.0 0.3 collective-permute-start.29
  149.3 1.4 collective-permute-start.30
  150.7 1.5 collective-permute-start.31
  152.3 11.9 %project.2 = (bf16[160,384]{1,0:T(8,128)(2,1)}, bf16[160,384]{1,0:T(8,128)(2,1)}, bf16[160,384]{1,0:T(8,128)(2,1)}, bf16[160,384]{1,0:T(8,128)(2,1)}, bf16[160,3...) custom-call(s32[1]{0:T(128)} %bitcast.place_ref, ...), custom_call_target="tpu_custom_call" | custom-call | flops 4026531840 | bytes 10485760 | tf_op jit(solution)/shard_map/project/pallas_call | solution.py:186
  164.1 0.2 collective-permute-start.21
  164.4 0.5 collective-permute-start.22
  165.0 2.6 %collective-permute-start.33 = (bf16[160,256]{1,0:T(8,128)(2,1)S(1)}, bf16[160,256]{1,0:T(8,128)(2,1)S(1)}, u32[]{:S(2)}, u32[]{:S(2)}) collective-permute-start(bf16[160,256]{1,0:T(8,128)(2,1)S(1)} %copy-done.38), channel_id=1, source_target_pairs={{0,24},{4,28},{8,16},{12,20},{16,8},{20,12},{24,0},{28,4},{1,25},{... | collective-permute-start | bytes 245768 | tf_op jit(solution)/shard_map/ppermute | solution.py:23
  167.8 1.6 collective-permute-done.32.refs_13_
  169.5 4.7 %collective-permute-start.23 = (bf16[160,384]{1,0:T(8,128)(2,1)}, bf16[160,384]{1,0:T(8,128)(2,1)S(1)}, u32[]{:S(2)}, u32[]{:S(2)}) collective-permute-start(bf16[160,384]{1,0:T(8,128)(2,1)} %get-tuple-element.45), channel_id=1, source_target_pairs={{0,12},{4,8},{8,4},{12,0},{16,28},{20,24},{24,20},{28,16},{1,13},{... | collective-permute-start | bytes 368648 | tf_op jit(solution)/shard_map/ppermute | solution.py:23
  174.2 1.8 collective-permute-start.25
  176.1 2.5 %collective-permute-start.27 = (bf16[160,384]{1,0:T(8,128)(2,1)}, bf16[160,384]{1,0:T(8,128)(2,1)S(1)}, u32[]{:S(2)}, u32[]{:S(2)}) collective-permute-start(bf16[160,384]{1,0:T(8,128)(2,1)} %get-tuple-element.49), channel_id=1, source_target_pairs={{0,28},{4,24},{8,20},{12,16},{16,12},{20,8},{24,4},{28,0},{1,29},{... | collective-permute-start | bytes 368648 | tf_op jit(solution)/shard_map/ppermute | solution.py:23
  178.6 7.2 %collective-permute-done.24.refs_4_ = bf16[160,384]{1,0:T(8,128)(2,1)S(1)} collective-permute-done((bf16[160,384]{1,0:T(8,128)(2,1)}, bf16[160,384]{1,0:T(8,128)(2,1)S(1)}, u32[]{:S(2)}, u32[]{:S(2)}) %collective-permute-start.24) | collective-permute-done | bytes 122912 | tf_op jit(solution)/shard_map/ppermute | solution.py:23
  185.8 1.7 collective-permute-done.25.refs_5_
  187.6 0.5 copy-done.19
  188.2 4.2 %assemble.1 = bf16[160,5120]{1,0:T(8,128)(2,1)} custom-call(s32[1]{0:T(128)} %bitcast.place_ref, f32[160,1]{1,0:T(8,128)} %fusion.5.valid_ref, bf16[160,384]{1,0:T(8,128)(2,1)} %get-tuple-element.42.refs_0_, bf16[160,384]{1,0:T(8,128)(2,1)} %copy-done.15, bf16[160,384]{1,0:T(8,128)(2,1)} %copy-done.16, bf16[160,384]{1,0:T(8,128)(2,1)} %copy-done.17, ...), custom_call_target="tpu_custom_call" | custom-call | bytes 3276800 | tf_op jit(solution)/shard_map/assemble/pallas_call | solution.py:234
  (119 shorter events, 1.5 us)
Async XLA Ops:
  6.5 132.4 %all-gather.5.cloned.1.call-start = ((), (), s32[]{:S(2)}) async-start(), calls=%async_computation.1 | async-start | bytes 2621440 | tf_op jit(solution)/shard_map/all_gather | solution.py:275
  10.6 141.7 %all-gather.3.cloned.1.call-start = ((), (), s32[]{:S(2)}) async-start(), calls=%async_computation | async-start | bytes 3932160 | tf_op jit(solution)/shard_map/all_gather | solution.py:275
  18.5 4.9 %collective-permute-start = (bf16[3,160,512]{2,1,0:T(8,128)(2,1)}, bf16[3,160,512]{2,1,0:T(8,128)(2,1)S(1)}, u32[]{:S(2)}, u32[]{:S(2)}) collective-permute-start(bf16[3,160,512]{2,1,0:T(8,128)(2,1)} %get-tuple-element.34), channel_id=1, source_target_pairs={{0,4},{4,0},{8,12},{12,8},{16,20},{20,16},{24,28},{28,24},{1,5},{5... | collective-permute-start | bytes 1474568 | tf_op jit(solution)/shard_map/ppermute | solution.py:23
  19.0 14.8 %collective-permute-start.1 = (bf16[3,160,512]{2,1,0:T(8,128)(2,1)}, bf16[3,160,512]{2,1,0:T(8,128)(2,1)S(1)}, u32[]{:S(2)}, u32[]{:S(2)}) collective-permute-start(bf16[3,160,512]{2,1,0:T(8,128)(2,1)} %get-tuple-element.35), channel_id=1, source_target_pairs={{0,8},{4,12},{8,0},{12,4},{16,24},{20,28},{24,16},{28,20},{1,9},{5... | collective-permute-start | bytes 1474568 | tf_op jit(solution)/shard_map/ppermute | solution.py:23
  21.6 22.4 %collective-permute-start.2 = (bf16[3,160,512]{2,1,0:T(8,128)(2,1)}, bf16[3,160,512]{2,1,0:T(8,128)(2,1)S(1)}, u32[]{:S(2)}, u32[]{:S(2)}) collective-permute-start(bf16[3,160,512]{2,1,0:T(8,128)(2,1)} %get-tuple-element.36), channel_id=1, source_target_pairs={{0,12},{4,8},{8,4},{12,0},{16,28},{20,24},{24,20},{28,16},{1,13},{... | collective-permute-start | bytes 1474568 | tf_op jit(solution)/shard_map/ppermute | solution.py:23
  21.7 22.3 %collective-permute-start.3 = (bf16[3,160,512]{2,1,0:T(8,128)(2,1)}, bf16[3,160,512]{2,1,0:T(8,128)(2,1)S(1)}, u32[]{:S(2)}, u32[]{:S(2)}) collective-permute-start(bf16[3,160,512]{2,1,0:T(8,128)(2,1)} %get-tuple-element.37), channel_id=1, source_target_pairs={{0,16},{4,20},{8,24},{12,28},{16,0},{20,4},{24,8},{28,12},{1,17},{... | collective-permute-start | bytes 1474568 | tf_op jit(solution)/shard_map/ppermute | solution.py:23
  23.4 42.9 %collective-permute-start.4 = (bf16[3,160,512]{2,1,0:T(8,128)(2,1)}, bf16[3,160,512]{2,1,0:T(8,128)(2,1)S(1)}, u32[]{:S(2)}, u32[]{:S(2)}) collective-permute-start(bf16[3,160,512]{2,1,0:T(8,128)(2,1)} %get-tuple-element.38), channel_id=1, source_target_pairs={{0,20},{4,16},{8,28},{12,24},{16,4},{20,0},{24,12},{28,8},{1,21},{... | collective-permute-start | bytes 1474568 | tf_op jit(solution)/shard_map/ppermute | solution.py:23
  23.4 42.9 %copy-start.30 = (bf16[3,160,512]{2,1,0:T(8,128)(2,1)}, bf16[3,160,512]{2,1,0:T(8,128)(2,1)S(1)}, u32[]{:S(2)}) copy-start(bf16[3,160,512]{2,1,0:T(8,128)(2,1)S(1)} %collective-permute-done.refs_1_) | copy-start | bytes 1474564
  23.4 42.9 %collective-permute-start.5 = (bf16[3,160,512]{2,1,0:T(8,128)(2,1)}, bf16[3,160,512]{2,1,0:T(8,128)(2,1)S(1)}, u32[]{:S(2)}, u32[]{:S(2)}) collective-permute-start(bf16[3,160,512]{2,1,0:T(8,128)(2,1)} %get-tuple-element.39), channel_id=1, source_target_pairs={{0,24},{4,28},{8,16},{12,20},{16,8},{20,12},{24,0},{28,4},{1,25},{... | collective-permute-start | bytes 1474568 | tf_op jit(solution)/shard_map/ppermute | solution.py:23
  33.9 32.5 %copy-start.31 = (bf16[3,160,512]{2,1,0:T(8,128)(2,1)}, bf16[3,160,512]{2,1,0:T(8,128)(2,1)S(1)}, u32[]{:S(2)}) copy-start(bf16[3,160,512]{2,1,0:T(8,128)(2,1)S(1)} %collective-permute-done.1.refs_2_) | copy-start | bytes 1474564
  33.9 32.5 %collective-permute-start.6 = (bf16[3,160,512]{2,1,0:T(8,128)(2,1)}, bf16[3,160,512]{2,1,0:T(8,128)(2,1)S(1)}, u32[]{:S(2)}, u32[]{:S(2)}) collective-permute-start(bf16[3,160,512]{2,1,0:T(8,128)(2,1)} %get-tuple-element.40), channel_id=1, source_target_pairs={{0,28},{4,24},{8,20},{12,16},{16,12},{20,8},{24,4},{28,0},{1,29},{... | collective-permute-start | bytes 1474568 | tf_op jit(solution)/shard_map/ppermute | solution.py:23
  88.3 50.7 %copy-start = (bf16[4,160,512]{2,1,0:T(8,128)(2,1)}, bf16[4,160,512]{2,1,0:T(8,128)(2,1)S(1)}, u32[]{:S(2)}) copy-start(bf16[4,160,512]{2,1,0:T(8,128)(2,1)S(1)} %get-tuple-element.59.refs_1_) | copy-start | bytes 1966084
  88.3 50.7 %copy-start.1 = (bf16[4,160,512]{2,1,0:T(8,128)(2,1)}, bf16[4,160,512]{2,1,0:T(8,128)(2,1)S(1)}, u32[]{:S(2)}) copy-start(bf16[4,160,512]{2,1,0:T(8,128)(2,1)S(1)} %get-tuple-element.60.refs_0_) | copy-start | bytes 1966084
  88.3 4.3 %collective-permute-start.7 = (bf16[4,160,512]{2,1,0:T(8,128)(2,1)S(1)}, bf16[4,160,512]{2,1,0:T(8,128)(2,1)S(1)}, u32[]{:S(2)}, u32[]{:S(2)}) collective-permute-start(bf16[4,160,512]{2,1,0:T(8,128)(2,1)S(1)} %get-tuple-element.60.refs_0_), channel_id=1, source_target_pairs={{0,4},{4,0},{8,12},{12,8},{16,20},{20,16},{24,28},{28,24},{1,5},{5... | collective-permute-start | bytes 1966088 | tf_op jit(solution)/shard_map/ppermute | solution.py:23
  88.8 17.6 %collective-permute-start.9 = (bf16[4,160,512]{2,1,0:T(8,128)(2,1)S(1)}, bf16[4,160,512]{2,1,0:T(8,128)(2,1)S(1)}, u32[]{:S(2)}, u32[]{:S(2)}) collective-permute-start(bf16[4,160,512]{2,1,0:T(8,128)(2,1)S(1)} %get-tuple-element.60.refs_0_), channel_id=1, source_target_pairs={{0,8},{4,12},{8,0},{12,4},{16,24},{20,28},{24,16},{28,20},{1,9},{5... | collective-permute-start | bytes 1966088 | tf_op jit(solution)/shard_map/ppermute | solution.py:23
  90.5 15.9 %collective-permute-start.8 = (bf16[4,160,512]{2,1,0:T(8,128)(2,1)S(1)}, bf16[4,160,512]{2,1,0:T(8,128)(2,1)S(1)}, u32[]{:S(2)}, u32[]{:S(2)}) collective-permute-start(bf16[4,160,512]{2,1,0:T(8,128)(2,1)S(1)} %get-tuple-element.59.refs_1_), channel_id=1, source_target_pairs={{0,4},{4,0},{8,12},{12,8},{16,20},{20,16},{24,28},{28,24},{1,5},{5... | collective-permute-start | bytes 1966088 | tf_op jit(solution)/shard_map/ppermute | solution.py:23
  90.5 17.7 %collective-permute-start.14 = (bf16[4,160,512]{2,1,0:T(8,128)(2,1)S(1)}, bf16[4,160,512]{2,1,0:T(8,128)(2,1)S(1)}, u32[]{:S(2)}, u32[]{:S(2)}) collective-permute-start(bf16[4,160,512]{2,1,0:T(8,128)(2,1)S(1)} %get-tuple-element.59.refs_1_), channel_id=1, source_target_pairs={{0,16},{4,20},{8,24},{12,28},{16,0},{20,4},{24,8},{28,12},{1,17},{... | collective-permute-start | bytes 1966088 | tf_op jit(solution)/shard_map/ppermute | solution.py:23
  92.1 28.4 %collective-permute-start.10 = (bf16[4,160,512]{2,1,0:T(8,128)(2,1)S(1)}, bf16[4,160,512]{2,1,0:T(8,128)(2,1)S(1)}, u32[]{:S(2)}, u32[]{:S(2)}) collective-permute-start(bf16[4,160,512]{2,1,0:T(8,128)(2,1)S(1)} %get-tuple-element.59.refs_1_), channel_id=1, source_target_pairs={{0,8},{4,12},{8,0},{12,4},{16,24},{20,28},{24,16},{28,20},{1,9},{5... | collective-permute-start | bytes 1966088 | tf_op jit(solution)/shard_map/ppermute | solution.py:23
  92.6 46.4 %copy-start.2 = (bf16[4,160,512]{2,1,0:T(8,128)(2,1)}, bf16[4,160,512]{2,1,0:T(8,128)(2,1)S(1)}, u32[]{:S(2)}) copy-start(bf16[4,160,512]{2,1,0:T(8,128)(2,1)S(1)} %collective-permute-done.7.refs_2_) | copy-start | bytes 1966084
  92.6 29.5 %collective-permute-start.13 = (bf16[4,160,512]{2,1,0:T(8,128)(2,1)S(1)}, bf16[4,160,512]{2,1,0:T(8,128)(2,1)S(1)}, u32[]{:S(2)}, u32[]{:S(2)}) collective-permute-start(bf16[4,160,512]{2,1,0:T(8,128)(2,1)S(1)} %get-tuple-element.60.refs_0_), channel_id=1, source_target_pairs={{0,16},{4,20},{8,24},{12,28},{16,0},{20,4},{24,8},{28,12},{1,17},{... | collective-permute-start | bytes 1966088 | tf_op jit(solution)/shard_map/ppermute | solution.py:23
  106.4 32.6 %copy-start.3 = (bf16[4,160,512]{2,1,0:T(8,128)(2,1)}, bf16[4,160,512]{2,1,0:T(8,128)(2,1)S(1)}, u32[]{:S(2)}) copy-start(bf16[4,160,512]{2,1,0:T(8,128)(2,1)S(1)} %collective-permute-done.9.refs_4_) | copy-start | bytes 1966084
  106.4 15.7 %collective-permute-start.11 = (bf16[4,160,512]{2,1,0:T(8,128)(2,1)S(1)}, bf16[4,160,512]{2,1,0:T(8,128)(2,1)S(1)}, u32[]{:S(2)}, u32[]{:S(2)}) collective-permute-start(bf16[4,160,512]{2,1,0:T(8,128)(2,1)S(1)} %collective-permute-done.9.refs_4_), channel_id=1, source_target_pairs={{0,4},{4,0},{8,12},{12,8},{16,20},{20,16},{24,28},{28,24},{1,5},{5... | collective-permute-start | bytes 1966088 | tf_op jit(solution)/shard_map/ppermute | solution.py:23
  106.4 32.6 %copy-start.4 = (bf16[4,160,512]{2,1,0:T(8,128)(2,1)}, bf16[4,160,512]{2,1,0:T(8,128)(2,1)S(1)}, u32[]{:S(2)}) copy-start(bf16[4,160,512]{2,1,0:T(8,128)(2,1)S(1)} %collective-permute-done.8.refs_3_) | copy-start | bytes 1966084
  106.4 29.3 %collective-permute-start.17 = (bf16[4,160,512]{2,1,0:T(8,128)(2,1)S(1)}, bf16[4,160,512]{2,1,0:T(8,128)(2,1)S(1)}, u32[]{:S(2)}, u32[]{:S(2)}) collective-permute-start(bf16[4,160,512]{2,1,0:T(8,128)(2,1)S(1)} %collective-permute-done.9.refs_4_), channel_id=1, source_target_pairs={{0,16},{4,20},{8,24},{12,28},{16,0},{20,4},{24,8},{28,12},{1,17},{... | collective-permute-start | bytes 1966088 | tf_op jit(solution)/shard_map/ppermute | solution.py:23
  108.3 27.5 %copy-start.5 = (bf16[4,160,512]{2,1,0:T(8,128)(2,1)}, bf16[4,160,512]{2,1,0:T(8,128)(2,1)S(1)}, u32[]{:S(2)}) copy-start(bf16[4,160,512]{2,1,0:T(8,128)(2,1)S(1)} %collective-permute-done.14.refs_9_) | copy-start | bytes 1966084
  108.3 27.5 %collective-permute-start.18 = (bf16[4,160,512]{2,1,0:T(8,128)(2,1)S(1)}, bf16[4,160,512]{2,1,0:T(8,128)(2,1)S(1)}, u32[]{:S(2)}, u32[]{:S(2)}) collective-permute-start(bf16[4,160,512]{2,1,0:T(8,128)(2,1)S(1)} %collective-permute-done.14.refs_9_), channel_id=1, source_target_pairs={{0,8},{4,12},{8,0},{12,4},{16,24},{20,28},{24,16},{28,20},{1,9},{5... | collective-permute-start | bytes 1966088 | tf_op jit(solution)/shard_map/ppermute | solution.py:23
  120.5 15.9 %collective-permute-start.16 = (bf16[4,160,512]{2,1,0:T(8,128)(2,1)S(1)}, bf16[4,160,512]{2,1,0:T(8,128)(2,1)S(1)}, u32[]{:S(2)}, u32[]{:S(2)}) collective-permute-start(bf16[4,160,512]{2,1,0:T(8,128)(2,1)S(1)} %collective-permute-done.14.refs_9_), channel_id=1, source_target_pairs={{0,4},{4,0},{8,12},{12,8},{16,20},{20,16},{24,28},{28,24},{1,5},{5... | collective-permute-start | bytes 1966088 | tf_op jit(solution)/shard_map/ppermute | solution.py:23
  122.1 14.2 %collective-permute-start.12 = (bf16[4,160,512]{2,1,0:T(8,128)(2,1)S(1)}, bf16[4,160,512]{2,1,0:T(8,128)(2,1)S(1)}, u32[]{:S(2)}, u32[]{:S(2)}) collective-permute-start(bf16[4,160,512]{2,1,0:T(8,128)(2,1)S(1)} %collective-permute-done.10.refs_5_), channel_id=1, source_target_pairs={{0,4},{4,0},{8,12},{12,8},{16,20},{20,16},{24,28},{28,24},{1,5},{5... | collective-permute-start | bytes 1966088 | tf_op jit(solution)/shard_map/ppermute | solution.py:23
  122.1 14.2 %collective-permute-start.15 = (bf16[4,160,512]{2,1,0:T(8,128)(2,1)S(1)}, bf16[4,160,512]{2,1,0:T(8,128)(2,1)S(1)}, u32[]{:S(2)}, u32[]{:S(2)}) collective-permute-start(bf16[4,160,512]{2,1,0:T(8,128)(2,1)S(1)} %collective-permute-done.13.refs_8_), channel_id=1, source_target_pairs={{0,4},{4,0},{8,12},{12,8},{16,20},{20,16},{24,28},{28,24},{1,5},{5... | collective-permute-start | bytes 1966088 | tf_op jit(solution)/shard_map/ppermute | solution.py:23
  135.8 2.1 %collective-permute-start.19 = (bf16[4,160,512]{2,1,0:T(8,128)(2,1)S(1)}, bf16[4,160,512]{2,1,0:T(8,128)(2,1)S(1)}, u32[]{:S(2)}, u32[]{:S(2)}) collective-permute-start(bf16[4,160,512]{2,1,0:T(8,128)(2,1)S(1)} %collective-permute-done.17.refs_12_), channel_id=1, source_target_pairs={{0,4},{4,0},{8,12},{12,8},{16,20},{20,16},{24,28},{28,24},{1,5},{5... | collective-permute-start | bytes 1966088 | tf_op jit(solution)/shard_map/ppermute | solution.py:23
  135.8 3.1 %collective-permute-start.20 = (bf16[4,160,512]{2,1,0:T(8,128)(2,1)S(1)}, bf16[4,160,512]{2,1,0:T(8,128)(2,1)}, u32[]{:S(2)}, u32[]{:S(2)}) collective-permute-start(bf16[4,160,512]{2,1,0:T(8,128)(2,1)S(1)} %collective-permute-done.18.refs_13_), channel_id=1, source_target_pairs={{0,4},{4,0},{8,12},{12,8},{16,20},{20,16},{24,28},{28,24},{1,5},{5... | collective-permute-start | bytes 1966088 | tf_op jit(solution)/shard_map/ppermute | solution.py:23
  148.8 15.6 %collective-permute-start.28 = (bf16[160,256]{1,0:T(8,128)(2,1)}, bf16[160,256]{1,0:T(8,128)(2,1)S(1)}, u32[]{:S(2)}, u32[]{:S(2)}) collective-permute-start(bf16[160,256]{1,0:T(8,128)(2,1)} %get-tuple-element.52), channel_id=1, source_target_pairs={{0,4},{4,0},{8,12},{12,8},{16,20},{20,16},{24,28},{28,24},{1,5},{5... | collective-permute-start | bytes 245768 | tf_op jit(solution)/shard_map/ppermute | solution.py:23
  149.0 15.9 %collective-permute-start.29 = (bf16[160,256]{1,0:T(8,128)(2,1)}, bf16[160,256]{1,0:T(8,128)(2,1)S(1)}, u32[]{:S(2)}, u32[]{:S(2)}) collective-permute-start(bf16[160,256]{1,0:T(8,128)(2,1)} %get-tuple-element.53), channel_id=1, source_target_pairs={{0,8},{4,12},{8,0},{12,4},{16,24},{20,28},{24,16},{28,20},{1,9},{5... | collective-permute-start | bytes 245768 | tf_op jit(solution)/shard_map/ppermute | solution.py:23
  149.3 15.7 %collective-permute-start.30 = (bf16[160,256]{1,0:T(8,128)(2,1)}, bf16[160,256]{1,0:T(8,128)(2,1)S(1)}, u32[]{:S(2)}, u32[]{:S(2)}) collective-permute-start(bf16[160,256]{1,0:T(8,128)(2,1)} %get-tuple-element.54), channel_id=1, source_target_pairs={{0,12},{4,8},{8,4},{12,0},{16,28},{20,24},{24,20},{28,16},{1,13},{... | collective-permute-start | bytes 245768 | tf_op jit(solution)/shard_map/ppermute | solution.py:23
  150.7 16.9 %collective-permute-start.31 = (bf16[160,256]{1,0:T(8,128)(2,1)}, bf16[160,256]{1,0:T(8,128)(2,1)S(1)}, u32[]{:S(2)}, u32[]{:S(2)}) collective-permute-start(bf16[160,256]{1,0:T(8,128)(2,1)} %get-tuple-element.55), channel_id=1, source_target_pairs={{0,16},{4,20},{8,24},{12,28},{16,0},{20,4},{24,8},{28,12},{1,17},{... | collective-permute-start | bytes 245768 | tf_op jit(solution)/shard_map/ppermute | solution.py:23
  164.1 11.9 %collective-permute-start.21 = (bf16[160,384]{1,0:T(8,128)(2,1)}, bf16[160,384]{1,0:T(8,128)(2,1)S(1)}, u32[]{:S(2)}, u32[]{:S(2)}) collective-permute-start(bf16[160,384]{1,0:T(8,128)(2,1)} %get-tuple-element.43), channel_id=1, source_target_pairs={{0,4},{4,0},{8,12},{12,8},{16,20},{20,16},{24,28},{28,24},{1,5},{5... | collective-permute-start | bytes 368648 | tf_op jit(solution)/shard_map/ppermute | solution.py:23
  164.4 23.1 %copy-start.22 = (bf16[160,256]{1,0:T(8,128)(2,1)}, bf16[160,256]{1,0:T(8,128)(2,1)S(1)}, u32[]{:S(2)}) copy-start(bf16[160,256]{1,0:T(8,128)(2,1)S(1)} %collective-permute-done.28.refs_9_) | copy-start | bytes 245764
  164.4 11.8 %collective-permute-start.22 = (bf16[160,384]{1,0:T(8,128)(2,1)}, bf16[160,384]{1,0:T(8,128)(2,1)S(1)}, u32[]{:S(2)}, u32[]{:S(2)}) collective-permute-start(bf16[160,384]{1,0:T(8,128)(2,1)} %get-tuple-element.44), channel_id=1, source_target_pairs={{0,8},{4,12},{8,0},{12,4},{16,24},{20,28},{24,16},{28,20},{1,9},{5... | collective-permute-start | bytes 368648 | tf_op jit(solution)/shard_map/ppermute | solution.py:23
  164.9 22.6 %copy-start.23 = (bf16[160,256]{1,0:T(8,128)(2,1)}, bf16[160,256]{1,0:T(8,128)(2,1)S(1)}, u32[]{:S(2)}) copy-start(bf16[160,256]{1,0:T(8,128)(2,1)S(1)} %collective-permute-done.29.refs_10_) | copy-start | bytes 245764
  164.9 4.6 %collective-permute-start.32 = (bf16[160,256]{1,0:T(8,128)(2,1)S(1)}, bf16[160,256]{1,0:T(8,128)(2,1)S(1)}, u32[]{:S(2)}, u32[]{:S(2)}) collective-permute-start(bf16[160,256]{1,0:T(8,128)(2,1)S(1)} %copy-done.39), channel_id=1, source_target_pairs={{0,20},{4,16},{8,28},{12,24},{16,4},{20,0},{24,12},{28,8},{1,21},{... | collective-permute-start | bytes 245768 | tf_op jit(solution)/shard_map/ppermute | solution.py:23
  165.0 22.5 %copy-start.24 = (bf16[160,256]{1,0:T(8,128)(2,1)}, bf16[160,256]{1,0:T(8,128)(2,1)S(1)}, u32[]{:S(2)}) copy-start(bf16[160,256]{1,0:T(8,128)(2,1)S(1)} %collective-permute-done.30.refs_11_) | copy-start | bytes 245764
  165.0 9.2 %collective-permute-start.33 = (bf16[160,256]{1,0:T(8,128)(2,1)S(1)}, bf16[160,256]{1,0:T(8,128)(2,1)S(1)}, u32[]{:S(2)}, u32[]{:S(2)}) collective-permute-start(bf16[160,256]{1,0:T(8,128)(2,1)S(1)} %copy-done.38), channel_id=1, source_target_pairs={{0,24},{4,28},{8,16},{12,20},{16,8},{20,12},{24,0},{28,4},{1,25},{... | collective-permute-start | bytes 245768 | tf_op jit(solution)/shard_map/ppermute | solution.py:23
  167.7 6.5 %collective-permute-start.34 = (bf16[160,256]{1,0:T(8,128)(2,1)S(1)}, bf16[160,256]{1,0:T(8,128)(2,1)S(1)}, u32[]{:S(2)}, u32[]{:S(2)}) collective-permute-start(bf16[160,256]{1,0:T(8,128)(2,1)S(1)} %copy-done.37), channel_id=1, source_target_pairs={{0,28},{4,24},{8,20},{12,16},{16,12},{20,8},{24,4},{28,0},{1,29},{... | collective-permute-start | bytes 245768 | tf_op jit(solution)/shard_map/ppermute | solution.py:23
  169.5 9.1 %collective-permute-start.23 = (bf16[160,384]{1,0:T(8,128)(2,1)}, bf16[160,384]{1,0:T(8,128)(2,1)S(1)}, u32[]{:S(2)}, u32[]{:S(2)}) collective-permute-start(bf16[160,384]{1,0:T(8,128)(2,1)} %get-tuple-element.45), channel_id=1, source_target_pairs={{0,12},{4,8},{8,4},{12,0},{16,28},{20,24},{24,20},{28,16},{1,13},{... | collective-permute-start | bytes 368648 | tf_op jit(solution)/shard_map/ppermute | solution.py:23
  174.2 11.6 %collective-permute-start.24 = (bf16[160,384]{1,0:T(8,128)(2,1)}, bf16[160,384]{1,0:T(8,128)(2,1)S(1)}, u32[]{:S(2)}, u32[]{:S(2)}) collective-permute-start(bf16[160,384]{1,0:T(8,128)(2,1)} %get-tuple-element.46), channel_id=1, source_target_pairs={{0,16},{4,20},{8,24},{12,28},{16,0},{20,4},{24,8},{28,12},{1,17},{... | collective-permute-start | bytes 368648 | tf_op jit(solution)/shard_map/ppermute | solution.py:23
  174.2 13.3 %collective-permute-start.25 = (bf16[160,384]{1,0:T(8,128)(2,1)}, bf16[160,384]{1,0:T(8,128)(2,1)S(1)}, u32[]{:S(2)}, u32[]{:S(2)}) collective-permute-start(bf16[160,384]{1,0:T(8,128)(2,1)} %get-tuple-element.47), channel_id=1, source_target_pairs={{0,20},{4,16},{8,28},{12,24},{16,4},{20,0},{24,12},{28,8},{1,21},{... | collective-permute-start | bytes 368648 | tf_op jit(solution)/shard_map/ppermute | solution.py:23
  176.0 11.5 %collective-permute-start.26 = (bf16[160,384]{1,0:T(8,128)(2,1)}, bf16[160,384]{1,0:T(8,128)(2,1)S(1)}, u32[]{:S(2)}, u32[]{:S(2)}) collective-permute-start(bf16[160,384]{1,0:T(8,128)(2,1)} %get-tuple-element.48), channel_id=1, source_target_pairs={{0,24},{4,28},{8,16},{12,20},{16,8},{20,12},{24,0},{28,4},{1,25},{... | collective-permute-start | bytes 368648 | tf_op jit(solution)/shard_map/ppermute | solution.py:23
  176.1 11.4 %collective-permute-start.27 = (bf16[160,384]{1,0:T(8,128)(2,1)}, bf16[160,384]{1,0:T(8,128)(2,1)S(1)}, u32[]{:S(2)}, u32[]{:S(2)}) collective-permute-start(bf16[160,384]{1,0:T(8,128)(2,1)} %get-tuple-element.49), channel_id=1, source_target_pairs={{0,28},{4,24},{8,20},{12,16},{16,12},{20,8},{24,4},{28,0},{1,29},{... | collective-permute-start | bytes 368648 | tf_op jit(solution)/shard_map/ppermute | solution.py:23
  (29 other events, 256.0 us)
Sparse Core Ops, SparseCore 0:
  10.7 48.6 all-gather.4
  60.9 62.2 all-gather.2

commit v3 on v2

v3 whole, which is shorter than its diff:
```python
import math

import jax
import jax.numpy as jnp
from jax import lax
from jax.experimental import pallas as pl
from jax.experimental.pallas import tpu as pltpu
from jax.sharding import PartitionSpec as P

HEAD_DIM = 128
BLOCK = 32
SENTINEL = 32.0
LIMIT = 24.0
VMEM = 56 * 1024 * 1024
QUERY_TILE = 256
UNIT = 128


def params(limit=VMEM):
    return pltpu.CompilerParams(vmem_limit_bytes=limit)


def order(count):
    return sorted(range(1, count), key=lambda mask: (mask == 1, mask & 1, -bin(mask).count("1")))


def variants(total):
    return sorted({-(-total * tenths // (10 * UNIT)) * UNIT for tenths in (4, 5, 6, 8, 10)})


def full_spec(shape):
    return pl.BlockSpec(shape, lambda i, *_: (0,) * len(shape))


def column_of(row):
    n = row.shape[1]
    diagonal = lax.broadcasted_iota(jnp.int32, (n, n), 0) == lax.broadcasted_iota(
        jnp.int32, (n, n), 1
    )
    return jnp.sum(jnp.where(diagonal, row, 0.0), axis=1, keepdims=True)


def valid_column(mask_ref, blocks):
    rows = mask_ref.shape[1]
    inside = lax.broadcasted_iota(jnp.int32, (1, rows), 1) < blocks * BLOCK
    return column_of(jnp.where((mask_ref[...] == 1) & inside, 1.0, 0.0))


def xor_permute(array, mask, count):
    return lax.ppermute(array, "cam", [(place, place ^ mask) for place in range(count)])


def pack(place, block_counts, row_mask, queries, keys, values, out_weight, sizes, count):
    _, rows, features = queries.shape
    width = features // count
    depth = out_weight.shape[0]
    columns = out_weight.shape[1] // count
    slicing = all(size % HEAD_DIM == 0 for size in sizes)
    chunks = len(sizes) if slicing else 0

    def body(place_ref, blocks_ref, mask_ref, q_ref, k_ref, v_ref, w_ref, *refs):
        out_refs = refs[:count]
        weight_refs = refs[count : count + chunks]
        key_in, key_out, key_sem, sems, weight_sems = refs[count + chunks :]
        load = pltpu.make_async_copy(k_ref.at[0], key_in, key_sem.at[0])
        load.start()
        copies = []
        for index in range(chunks):
            start = pl.multiple_of(place_ref[0] * columns + sum(sizes[:index]), HEAD_DIM)
            copy = pltpu.make_async_copy(
                w_ref.at[:, pl.ds(start, sizes[index])],
                weight_refs[index],
                weight_sems.at[index],
            )
            copy.start()
            copies.append(copy)
        starts = [pl.multiple_of((place_ref[0] ^ m) * width, HEAD_DIM) for m in range(count)]
        for mask in range(count):
            for slot, ref in ((0, q_ref), (2, v_ref)):
                copy = pltpu.make_async_copy(
                    ref.at[0, :, pl.ds(starts[mask], width)],
                    out_refs[mask].at[slot],
                    sems.at[mask, slot],
                )
                copy.start()
                copies.append(copy)
        good = valid_column(mask_ref, blocks_ref[0, 0]) > 0.5
        load.wait()
        for mask in range(count):
            part = key_in[:, pl.ds(starts[mask], width)]
            key_out[mask] = jnp.where(good, part, jnp.bfloat16(SENTINEL))
            copy = pltpu.make_async_copy(key_out.at[mask], out_refs[mask].at[1], sems.at[mask, 1])
            copy.start()
            copies.append(copy)
        for copy in copies:
            copy.wait()

    any_spec = pl.BlockSpec(memory_space=pl.ANY)
    weight_shapes = [
        jax.ShapeDtypeStruct((depth, size), jnp.bfloat16) for size in sizes[:chunks]
    ]
    outputs = pl.pallas_call(
        body,
        grid_spec=pltpu.PrefetchScalarGridSpec(
            num_scalar_prefetch=2,
            grid=(1,),
            in_specs=[full_spec((1, rows))] + [any_spec] * 4,
            out_specs=[any_spec] * (count + chunks),
            scratch_shapes=[
                pltpu.VMEM((rows, features), jnp.bfloat16),
                pltpu.VMEM((count, rows, width), jnp.bfloat16),
                pltpu.SemaphoreType.DMA((1,)),
                pltpu.SemaphoreType.DMA((count, 3)),
                pltpu.SemaphoreType.DMA((len(sizes),)),
            ],
        ),
        out_shape=[jax.ShapeDtypeStruct((3, rows, width), jnp.bfloat16)] * count + weight_shapes,
        compiler_params=params(),
        cost_estimate=pl.CostEstimate(
            flops=0, bytes_accessed=12 * rows * features, transcendentals=0
        ),
        name="pack",
    )(place, block_counts, row_mask, queries, keys, values, out_weight)
    weights = list(outputs[count:])
    if not slicing:
        for index, size in enumerate(sizes):
            start = place[0] * columns + sum(sizes[:index])
            weights.append(lax.dynamic_slice_in_dim(out_weight, start, size, axis=1))
    return list(outputs[:count]), weights


def packed_offsets(place_ref, counts_ref, table, count):
    by_mask, running = [], 0
    for mask in range(count):
        by_mask.append(running)
        table[mask] = running
        running = running + counts_ref[mask] * BLOCK
    by_view, position = [], 0
    for view in range(count):
        by_view.append(position)
        position = position + counts_ref[place_ref[0] ^ view] * BLOCK
    return by_mask, by_view, running


def rows_at(start, size):
    return pl.ds(start if isinstance(start, int) else pl.multiple_of(start, BLOCK), size)


def attend(place, counts, received, rows):
    count = len(received)
    width = received[0].shape[2]
    total = count * rows
    factor = math.log2(math.e) / math.sqrt(HEAD_DIM)

    def body(place_ref, counts_ref, *refs):
        parts = refs[:count]
        out_ref = refs[count]
        query_all, key_all, value_all, value_t, result, table = refs[count + 1 :]
        by_mask, by_view, used = packed_offsets(place_ref, counts_ref, table, count)

        @pl.when(pl.program_id(0) == 0)
        def _():
            value_all[...] = jnp.zeros_like(value_all)

        for mask in range(count):
            where = rows_at(by_mask[mask], rows)
            query_all[where, :] = parts[mask][0]
            key_all[where, :] = parts[mask][1]
            value_all[where, :] = parts[mask][2]
        key_all[rows_at(used, total // 5), :] = jnp.full(
            (total // 5, HEAD_DIM), SENTINEL, jnp.bfloat16
        )
        below = 0
        for size in variants(total):

            @pl.when((used > below) & (used <= size))
            def _(size=size):
                value_t[:, :size] = value_all[:size, :].T
                key_rows = key_all[:size, :]
                bias = jnp.where(key_rows.astype(jnp.float32) > LIMIT, jnp.float32(-1e30), 0.0)
                bias = jnp.concatenate([bias] * (QUERY_TILE // HEAD_DIM), axis=1)

                def tile(index, carry):
                    where = pl.ds(pl.multiple_of(index * QUERY_TILE, QUERY_TILE), QUERY_TILE)
                    scores = lax.dot_general(
                        key_rows,
                        query_all[where, :],
                        (((1,), (1,)), ((), ())),
                        preferred_element_type=jnp.float32,
                    )
                    scores = scores + bias
                    top = jnp.max(scores, axis=0, keepdims=True)
                    raised = jnp.exp2((scores - top) * factor)
                    norm = jnp.sum(raised, axis=0, keepdims=True)
                    summed = jnp.dot(
                        value_t[:, :size],
                        raised.astype(jnp.bfloat16),
                        preferred_element_type=jnp.float32,
                    )
                    result[where, :] = (summed / norm).T.astype(jnp.bfloat16)
                    return carry

                lax.fori_loop(0, (used + QUERY_TILE - 1) // QUERY_TILE, tile, 0)

            below = size
        for view in range(count):
            moved = result[rows_at(table[place_ref[0] ^ view], rows), :]
            out_ref[rows_at(by_view[view], rows), :] = moved

    flops = 4 * total * total * width // 4
    return pl.pallas_call(
        body,
        grid_spec=pltpu.PrefetchScalarGridSpec(
            num_scalar_prefetch=2,
            grid=(width // HEAD_DIM,),
            in_specs=[pl.BlockSpec((3, rows, HEAD_DIM), lambda h, *_: (0, 0, h))] * count,
            out_specs=pl.BlockSpec((total, HEAD_DIM), lambda h, *_: (0, h)),
            scratch_shapes=[
                pltpu.VMEM((total, HEAD_DIM), jnp.bfloat16),
                pltpu.VMEM((total + total // 5, HEAD_DIM), jnp.bfloat16),
                pltpu.VMEM((total, HEAD_DIM), jnp.bfloat16),
                pltpu.VMEM((HEAD_DIM, total), jnp.bfloat16),
                pltpu.VMEM((total, HEAD_DIM), jnp.bfloat16),
                pltpu.SMEM((count,), jnp.int32),
            ],
        ),
        out_shape=jax.ShapeDtypeStruct((total, width), jnp.bfloat16),
        compiler_params=params(),
        cost_estimate=pl.CostEstimate(
            flops=flops, bytes_accessed=8 * total * width, transcendentals=flops // 512
        ),
        name="attend",
    )(place, counts, *received)


def gather_features(own, count):
    half = own.shape[0] // 2
    held = {0: [own[:half], own[half:]]}
    if count == 8:
        over_x_0 = xor_permute(held[0][0], 2, count)
        over_y_1 = xor_permute(held[0][1], 4, count)
        over_x_1 = xor_permute(held[0][1], 2, count)
        over_y_0 = xor_permute(held[0][0], 4, count)
        diagonal_0 = xor_permute(over_x_0, 4, count)
        diagonal_1 = xor_permute(over_y_1, 2, count)
        held[2] = [over_x_0, over_x_1]
        held[4] = [over_y_0, over_y_1]
        held[6] = [diagonal_0, diagonal_1]
    else:
        for mask in range(2, count, 2):
            held[mask] = [xor_permute(piece, mask, count) for piece in held[0]]
    for mask in range(0, count, 2):
        held[mask + 1] = [xor_permute(piece, 1, count) for piece in held[mask]]
    return [held[mask] for mask in range(count)]


def unfilled(shapes):
    def body(*refs):
        pass

    return pl.pallas_call(
        body,
        out_specs=[pl.BlockSpec(memory_space=pl.ANY)] * len(shapes),
        out_shape=shapes,
        name="unfilled",
    )()


def project(place, counts, features, weight, rows):
    count = len(features)
    pieces = len(features[0])
    lengths = [piece.shape[0] for piece in features[0]]
    width = features[0][0].shape[1]
    columns = weight.shape[1]
    total = count * rows
    bounds = [size for size in variants(total) if size <= lengths[0] + lengths[1]] + [total]

    def body(place_ref, counts_ref, *refs):
        flat = refs[: pieces * count]
        weight_ref = refs[pieces * count]
        out_refs = refs[pieces * count + 1 : (pieces + 1) * count + 1]
        landed, weight_all, sums, sems, weight_sems = refs[(pieces + 1) * count + 1 :]
        used = sum(counts_ref[mask] for mask in range(count)) * BLOCK
        weight_copies = []
        for mask in range(count):
            start = pl.multiple_of((place_ref[0] ^ mask) * width, width)
            copy = pltpu.make_async_copy(
                weight_ref.at[pl.ds(start, width), :], weight_all.at[mask], weight_sems.at[mask]
            )
            copy.start()
            weight_copies.append(copy)
        below = 0
        for size in bounds:

            @pl.when((used > below) & (used <= size))
            def _(size=size):
                copies = []
                for mask in range(count):
                    first = 0
                    for index in range(pieces):
                        length = min(lengths[index], size - first)
                        if length <= 0:
                            break
                        copy = pltpu.make_async_copy(
                            flat[pieces * mask + index].at[:length, :],
                            landed.at[mask, first : first + length, :],
                            sems.at[mask, index],
                        )
                        copy.start()
                        copies.append((mask, copy))
                        first += length
                for mask in range(count):
                    weight_copies[mask].wait()
                    for owner, copy in copies:
                        if owner == mask:
                            copy.wait()
                    part = jnp.dot(
                        landed[mask, :size, :],
                        weight_all[mask],
                        preferred_element_type=jnp.float32,
                    )
                    if mask == 0:
                        sums[:size, :] = part
                    else:
                        sums[:size, :] += part

            below = size
        for mask in range(count):
            position = 0
            for view in range(count):
                position = position + jnp.where(
                    view < (place_ref[0] ^ mask), counts_ref[place_ref[0] ^ view], 0
                )
            moved = sums[rows_at(position * BLOCK, rows), :]
            out_refs[mask][...] = moved.astype(jnp.bfloat16)

    any_spec = pl.BlockSpec(memory_space=pl.ANY)
    flat = [piece for group in features for piece in group]
    return pl.pallas_call(
        body,
        grid_spec=pltpu.PrefetchScalarGridSpec(
            num_scalar_prefetch=2,
            grid=(1,),
            in_specs=[any_spec] * (pieces * count + 1),
            out_specs=[full_spec((rows, columns))] * count,
            scratch_shapes=[
                pltpu.VMEM((count, total, width), jnp.bfloat16),
                pltpu.VMEM((count, width, columns), jnp.bfloat16),
                pltpu.VMEM((total, columns), jnp.float32),
                pltpu.SemaphoreType.DMA((count, pieces)),
                pltpu.SemaphoreType.DMA((count,)),
            ],
        ),
        out_shape=[jax.ShapeDtypeStruct((rows, columns), jnp.bfloat16)] * count,
        compiler_params=params(),
        cost_estimate=pl.CostEstimate(
            flops=total * count * width * columns,
            bytes_accessed=total * count * width,
            transcendentals=0,
        ),
        name="project",
    )(place, counts, *flat, weight)


def assemble(place, block_counts, row_mask, chunks, sizes, count):
    rows = row_mask.shape[1]
    columns = sum(sizes)
    if any(size % HEAD_DIM for size in sizes):
        joined = [
            jnp.concatenate([chunk[mask] for chunk in chunks], axis=1) for mask in range(count)
        ]
        stacked = jnp.stack(joined)[jnp.arange(count) ^ place[0]]
        result = jnp.moveaxis(stacked, 0, 1).reshape(rows, count * columns)
        offsets = jnp.arange(rows, dtype=jnp.int32)
        good = (row_mask[0] == 1) & (offsets // BLOCK < block_counts[0, 0])
        return jnp.where(good[:, None], result, jnp.bfloat16(0.0))

    def body(place_ref, blocks_ref, mask_ref, *refs):
        out_ref = refs[-1]
        good = valid_column(mask_ref, blocks_ref[0, 0]) > 0.5
        for index in range(len(sizes)):
            for mask in range(count):
                start = (place_ref[0] ^ mask) * columns + sum(sizes[:index])
                chosen = pl.ds(pl.multiple_of(start, HEAD_DIM), sizes[index])
                piece = refs[index * count + mask][...]
                out_ref[:, chosen] = jnp.where(good, piece, jnp.bfloat16(0.0))

    return pl.pallas_call(
        body,
        grid_spec=pltpu.PrefetchScalarGridSpec(
            num_scalar_prefetch=2,
            grid=(1,),
            in_specs=[full_spec((1, rows))]
            + [full_spec((rows, size)) for size in sizes for mask in range(count)],
            out_specs=full_spec((rows, count * columns)),
        ),
        out_shape=jax.ShapeDtypeStruct((rows, count * columns), jnp.bfloat16),
        compiler_params=params(),
        cost_estimate=pl.CostEstimate(
            flops=0, bytes_accessed=4 * rows * count * columns, transcendentals=0
        ),
        name="assemble",
    )(place, block_counts, row_mask, *[piece for chunk in chunks for piece in chunk])


def share_counts(block_counts, count):
    counts = block_counts[0]
    step = 1
    while step < count:
        counts = jnp.concatenate([counts, xor_permute(counts, step, count)])
        step *= 2
    most = jnp.sum(counts)[None]
    groups = lax.axis_size("fsdp")
    step = 1
    while step < groups:
        pairs = [(group, group ^ step) for group in range(groups)]
        most = jnp.maximum(most, lax.ppermute(most, "fsdp", pairs))
        step *= 2
    return counts, most[0]


def local(queries, keys, values, out_weight, block_counts, row_mask):
    rows = queries.shape[1]
    count = lax.axis_size("cam")
    total = count * rows
    place_array = jnp.full((1,), lax.axis_index("cam"), jnp.int32)
    columns = out_weight.shape[1] // count
    first = max(HEAD_DIM, -(-columns * 3 // 5 // HEAD_DIM) * HEAD_DIM)
    sizes = [first, columns - first]

    payloads, weights = pack(
        place_array, block_counts, row_mask, queries, keys, values, out_weight, sizes, count
    )
    weights = [lax.all_gather(part, "fsdp", axis=0, tiled=True) for part in weights]
    received = [payloads[0]] + [None] * (count - 1)
    for mask in order(count):
        received[mask] = xor_permute(payloads[mask], mask, count)
    counts, most = share_counts(block_counts, count)
    attended = attend(place_array, counts, received, rows)

    always = total * 3 // 5
    features = gather_features(attended[:always], count)
    rest = attended[always:]
    shapes = [jax.ShapeDtypeStruct((rest.shape[0] // 2, rest.shape[1]), rest.dtype)] * 2 * count
    more = lax.cond(
        most * BLOCK > always,
        lambda part: [piece for pair in gather_features(part, count) for piece in pair],
        lambda part: list(unfilled(shapes)),
        rest,
    )
    features = [features[mask] + more[2 * mask : 2 * mask + 2] for mask in range(count)]
    chunks = []
    for weight in weights:
        pieces = project(place_array, counts, features, weight, rows)
        chunk = [pieces[0]] + [None] * (count - 1)
        for mask in order(count):
            chunk[mask] = xor_permute(pieces[mask], mask, count)
        chunks.append(chunk)
    return assemble(place_array, block_counts, row_mask, chunks, sizes, count)[None]


def solution(mesh):
    in_specs = (
        P("fsdp", "cam", None),
        P("fsdp", "cam", None),
        P("fsdp", "cam", None),
        P("fsdp", None),
        P("fsdp", "cam"),
        P("fsdp", "cam"),
    )
    out_specs = P("fsdp", "cam", None)
    return jax.shard_map(local, mesh=mesh, in_specs=in_specs, out_specs=out_specs, check_vma=False)
```

time: 200 us -> 302 us (1.51)
  Pallas kernels: 50.9 us -> 152 us
  local copies, waits for them, and re-layouts: 8.29 us -> 2.72 us
  starting transfers between devices: 34.5 us -> 39.6 us
  waiting for transfers between devices: 90.4 us -> 86.7 us
  other arithmetic: 0.66 us -> 4.21 us
  between operations: 14.5 us -> 17.8 us
    pallas_call x1, Pallas kernels: 5.7 us -> 121 us  [pack(): pl.pallas_call(body, grid_spec=pltpu.PrefetchScalarGridSpec(num_scalar_pr...]
    pallas_call x1, Pallas kernels: 19.4 us -> 11.9 us  [attend(): pl.pallas_call(body, grid_spec=pltpu.PrefetchScalarGridSpec(num_scalar_pr...]
    ppermute x0 -> x2, starting transfers between devices: none -> 7.42 us  [share_counts(): most = jnp.maximum(most, lax.ppermute(most, 'fsdp', pairs))]
    pallas_call x2, Pallas kernels: 21.7 us -> 15.7 us  [project(): pl.pallas_call(body, grid_spec=pltpu.PrefetchScalarGridSpec(num_scalar_pr...]
    ppermute x35 -> x38, waiting for transfers between devices: 89.7 us -> 84.5 us  [xor_permute(): lax.ppermute(array, 'cam', [(place, place ^ mask) for place in range(coun...]
    dynamic_slice x2 -> x0, local copies, waits for them, and re-layouts: 4.02 us -> none  [local(): part = lax.dynamic_slice_in_dim(out_weight, start, size, axis=1)]
    ppermute x35 -> x38, starting transfers between devices: 34.5 us -> 32.1 us  [xor_permute(): lax.ppermute(array, 'cam', [(place, place ^ mask) for place in range(coun...]
  transfers between devices with their start and end apart: 37 -> 42, of which waited for: 12 -> 15; matrix products, arithmetic and copies ran while one was open for 1% -> 1% of each run, Pallas kernels for 23% -> 9%
where the time goes in v3:
time: 302 us; the launch traced here: 303 us
  Pallas kernels  152 us (50%)
  waiting for transfers between devices  86.7 us (29%)
  starting transfers between devices  39.6 us (13%)
  between operations  17.8 us (6%)
  other arithmetic  4.21 us (1%)
    pallas_call x1, Pallas kernels, pack(): pl.pallas_call(body, grid_spec=pltpu.PrefetchScalarGridSpec(num_scalar_pr...  121 us
    ppermute x38, waiting for transfers between devices, xor_permute(): lax.ppermute(array, 'cam', [(place, place ^ mask) for place in range(coun...  84.5 us
    ppermute x38, starting transfers between devices, xor_permute(): lax.ppermute(array, 'cam', [(place, place ^ mask) for place in range(coun...  32.1 us
    pallas_call x2, Pallas kernels, project(): pl.pallas_call(body, grid_spec=pltpu.PrefetchScalarGridSpec(num_scalar_pr...  15.7 us
    pallas_call x1, Pallas kernels, attend(): pl.pallas_call(body, grid_spec=pltpu.PrefetchScalarGridSpec(num_scalar_pr...  11.9 us
    ppermute x2, starting transfers between devices, share_counts(): most = jnp.maximum(most, lax.ppermute(most, 'fsdp', pairs))  7.42 us
  transfers between devices with their start and end apart: 42, of which 15 were waited for; matrix products, arithmetic and copies ran while one was open for 1% of the time, Pallas kernels for 9%

profile of v3, /device:TPU:0, one launch (start us, length us, event | category | flops | bytes accessed | tf_op | source)
XLA Modules:
  0.0 302.7 jit_solution(16579548262763862359)
XLA Ops:
  7.2 121.2 %pack.1 = (bf16[3,160,512]{2,1,0:T(8,128)(2,1)}, bf16[3,160,512]{2,1,0:T(8,128)(2,1)}, bf16[3,160,512]{2,1,0:T(8,128)(2,1)}, bf16[3,160,512]{2,1,0:T(8,128)(2,1)...) custom-call(s32[1]{0:T(128)} %bitcast.place_ref, ...), custom_call_target="tpu_custom_call" | custom-call | bytes 7864320 | tf_op jit(solution)/shard_map/pack/pallas_call | solution.py:102
  128.5 0.7 all-gather.3.cloned.1.call-update
  129.7 2.6 collective-permute-start.18
  132.4 2.0 collective-permute-start.20
  134.4 0.7 pad_add_fusion
  135.2 1.5 collective-permute-start.15
  137.3 17.5 %collective-permute-done.15 = s32[2]{0:T(128)S(1)} collective-permute-done((s32[2]{0:T(128)S(1)}, s32[2]{0:T(128)S(1)}, u32[]{:S(2)}, u32[]{:S(2)}) %collective-permute-start.15) | collective-permute-done | bytes 40 | tf_op jit(solution)/shard_map/ppermute | solution.py:50
  154.8 0.7 pad_add_fusion.1
  155.5 1.8 collective-permute-start.16
  157.3 0.7 reduce_sum.30
  159.1 0.7 reduce_sum.32
  160.5 3.2 %collective-permute-start.24 = (s32[1]{0:T(128)}, s32[1]{0:T(128)}, u32[]{:S(2)}, u32[]{:S(2)}) collective-permute-start(s32[1]{0:T(128)} %bitcast.4), channel_id=1, source_target_pairs={{0,1},{1,0},{2,3},{3,2},{4,5},{5,4},{6,7},{7,6},{8,9},{9,8},{10,11... | collective-permute-start | bytes 20 | tf_op jit(solution)/shard_map/ppermute | solution.py:417
  164.6 4.2 %collective-permute-start.25 = (s32[1]{0:T(128)}, s32[1]{0:T(128)}, u32[]{:S(2)}, u32[]{:S(2)}) collective-permute-start(s32[1]{0:T(128)} %max.6), channel_id=1, source_target_pairs={{0,2},{1,3},{2,0},{3,1},{4,6},{5,7},{6,4},{7,5},{8,10},{9,11},{10,... | collective-permute-start | bytes 20 | tf_op jit(solution)/shard_map/ppermute | solution.py:417
  168.8 1.1 collective-permute-done.25
  170.0 2.4 collective-permute-start.22
  172.5 1.5 collective-permute-start.23
  174.0 1.3 pad_add_fusion.2.counts_ref
  176.0 28.8 %collective-permute-done.21.refs_5_ = bf16[3,160,512]{2,1,0:T(8,128)(2,1)S(1)} collective-permute-done((bf16[3,160,512]{2,1,0:T(8,128)(2,1)}, bf16[3,160,512]{2,1,0:T(8,128)(2,1)S(1)}, u32[]{:S(2)}, u32[]{:S(2)}) %collective-permute-start.21) | collective-permute-done | bytes 491552 | tf_op jit(solution)/shard_map/ppermute | solution.py:50
  204.8 0.8 copy-done.19
  206.0 11.9 %attend.1 = bf16[1280,512]{1,0:T(8,128)(2,1)S(1)} custom-call(s32[1]{0:T(128)} %bitcast.place_ref, s32[8]{0:T(128)} %pad_add_fusion.2.counts_ref, bf16[3,160,512]{2,1,0:T(8,128)(2,1)} %get-tuple-element.49.refs_0_, bf16[3,160,512]{2,1,0:T(8,128)(2,1)} %copy-done.15, bf16[3,160,512]{2,1,0:T(8,128)(2,1)} %copy-done.16, bf16[3,160,512]{2,1,0:T(8,128)(2,1)} %copy-done.17, ...), custom_call_target="tpu_custom_call" | custom-call | flops 838860800 | bytes 5242880 | tf_op jit(solution)/shard_map/attend/pallas_call | solution.py:211
  218.3 1.5 collective-permute-start.28
  219.7 0.6 collective-permute-start.33
  220.3 0.6 collective-permute-start.29
  220.9 1.4 collective-permute-start.32
  222.3 7.9 %collective-permute-done.28.refs_8_ = bf16[384,512]{1,0:T(8,128)(2,1)S(1)} collective-permute-done((bf16[384,512]{1,0:T(8,128)(2,1)S(1)}, bf16[384,512]{1,0:T(8,128)(2,1)S(1)}, u32[]{:S(2)}, u32[]{:S(2)}) %collective-permute-start.28) | collective-permute-done | bytes 393248 | tf_op jit(solution)/shard_map/ppermute | solution.py:50
  230.7 1.0 collective-permute-done.33.refs_17_
  231.7 0.6 collective-permute-start.37
  232.2 6.4 %collective-permute-done.29.refs_9_ = bf16[384,512]{1,0:T(8,128)(2,1)S(1)} collective-permute-done((bf16[384,512]{1,0:T(8,128)(2,1)S(1)}, bf16[384,512]{1,0:T(8,128)(2,1)S(1)}, u32[]{:S(2)}, u32[]{:S(2)}) %collective-permute-start.29) | collective-permute-done | bytes 393248 | tf_op jit(solution)/shard_map/ppermute | solution.py:50
  238.7 1.4 collective-permute-done.32.refs_16_
  240.6 7.5 %collective-permute-done.36.refs_24_ = bf16[384,512]{1,0:T(8,128)(2,1)S(1)} collective-permute-done((bf16[384,512]{1,0:T(8,128)(2,1)S(1)}, bf16[384,512]{1,0:T(8,128)(2,1)S(1)}, u32[]{:S(2)}, u32[]{:S(2)}) %collective-permute-start.36) | collective-permute-done | bytes 393248 | tf_op jit(solution)/shard_map/ppermute | solution.py:50
  248.7 1.2 collective-permute-done.38.refs_28_
  249.9 0.8 copy-done.14
  250.7 7.7 %project.3 = (bf16[160,256]{1,0:T(8,128)(2,1)}, bf16[160,256]{1,0:T(8,128)(2,1)}, bf16[160,256]{1,0:T(8,128)(2,1)}, bf16[160,256]{1,0:T(8,128)(2,1)}, bf16[160,2...) custom-call(s32[1]{0:T(128)} %bitcast.place_ref, ...), custom_call_target="tpu_custom_call" | custom-call | flops 1342177280 | bytes 5242880 | tf_op jit(solution)/shard_map/project/pallas_call | solution.py:339
  258.7 0.6 collective-permute-start.48
  259.3 1.1 collective-permute-start.49
  260.8 7.9 %project.2 = (bf16[160,384]{1,0:T(8,128)(2,1)}, bf16[160,384]{1,0:T(8,128)(2,1)}, bf16[160,384]{1,0:T(8,128)(2,1)}, bf16[160,384]{1,0:T(8,128)(2,1)}, bf16[160,3...) custom-call(s32[1]{0:T(128)} %bitcast.place_ref, ...), custom_call_target="tpu_custom_call" | custom-call | flops 2013265920 | bytes 5242880 | tf_op jit(solution)/shard_map/project/pallas_call | solution.py:339
  269.0 0.6 collective-permute-start.41
  269.6 1.3 collective-permute-start.51
  270.9 1.4 collective-permute-start.52
  272.3 1.4 collective-permute-start.53
  274.1 1.2 collective-permute-start.42
  275.3 2.8 collective-permute-done.52.refs_14_
  278.2 2.3 collective-permute-start.43
  280.6 1.1 collective-permute-start.45
  281.7 1.2 collective-permute-start.46
  283.0 7.1 %collective-permute-done.43.refs_4_ = bf16[160,384]{1,0:T(8,128)(2,1)S(1)} collective-permute-done((bf16[160,384]{1,0:T(8,128)(2,1)}, bf16[160,384]{1,0:T(8,128)(2,1)S(1)}, u32[]{:S(2)}, u32[]{:S(2)}) %collective-permute-start.43) | collective-permute-done | bytes 122912 | tf_op jit(solution)/shard_map/ppermute | solution.py:50
  290.1 2.0 collective-permute-done.44.refs_5_
  292.9 3.0 assemble.1
  (133 shorter events, 5.9 us)
Async XLA Ops:
  6.5 244.1 %all-gather.5.cloned.1.call-start = ((), (), s32[]{:S(2)}) async-start(), calls=%async_computation.1 | async-start | bytes 2621440 | tf_op jit(solution)/shard_map/all_gather | solution.py:434
  128.4 41.7 %copy-start.37 = (bf16[3,160,512]{2,1,0:T(8,128)(2,1)S(1)}, bf16[3,160,512]{2,1,0:T(8,128)(2,1)}, u32[]{:S(2)}) copy-start(bf16[3,160,512]{2,1,0:T(8,128)(2,1)} %get-tuple-element.55) | copy-start | bytes 1474564
  128.4 44.1 %copy-start.36 = (bf16[3,160,512]{2,1,0:T(8,128)(2,1)S(1)}, bf16[3,160,512]{2,1,0:T(8,128)(2,1)}, u32[]{:S(2)}) copy-start(bf16[3,160,512]{2,1,0:T(8,128)(2,1)} %get-tuple-element.56) | copy-start | bytes 1474564
  128.4 132.4 %all-gather.3.cloned.1.call-start = ((), (), s32[]{:S(2)}) async-start(), calls=%async_computation | async-start | bytes 3932160 | tf_op jit(solution)/shard_map/all_gather | solution.py:434
  129.2 40.8 %collective-permute-start.17 = (bf16[3,160,512]{2,1,0:T(8,128)(2,1)}, bf16[3,160,512]{2,1,0:T(8,128)(2,1)S(1)}, u32[]{:S(2)}, u32[]{:S(2)}) collective-permute-start(bf16[3,160,512]{2,1,0:T(8,128)(2,1)} %get-tuple-element.50), channel_id=1, source_target_pairs={{0,4},{4,0},{8,12},{12,8},{16,20},{20,16},{24,28},{28,24},{1,5},{5... | collective-permute-start | bytes 1474568 | tf_op jit(solution)/shard_map/ppermute | solution.py:50
  129.7 42.8 %collective-permute-start.18 = (bf16[3,160,512]{2,1,0:T(8,128)(2,1)}, bf16[3,160,512]{2,1,0:T(8,128)(2,1)S(1)}, u32[]{:S(2)}, u32[]{:S(2)}) collective-permute-start(bf16[3,160,512]{2,1,0:T(8,128)(2,1)} %get-tuple-element.51), channel_id=1, source_target_pairs={{0,8},{4,12},{8,0},{12,4},{16,24},{20,28},{24,16},{28,20},{1,9},{5... | collective-permute-start | bytes 1474568 | tf_op jit(solution)/shard_map/ppermute | solution.py:50
  132.2 2.2 collective-permute-start.14
  132.4 43.5 %collective-permute-start.19 = (bf16[3,160,512]{2,1,0:T(8,128)(2,1)}, bf16[3,160,512]{2,1,0:T(8,128)(2,1)S(1)}, u32[]{:S(2)}, u32[]{:S(2)}) collective-permute-start(bf16[3,160,512]{2,1,0:T(8,128)(2,1)} %get-tuple-element.52), channel_id=1, source_target_pairs={{0,12},{4,8},{8,4},{12,0},{16,28},{20,24},{24,20},{28,16},{1,13},{... | collective-permute-start | bytes 1474568 | tf_op jit(solution)/shard_map/ppermute | solution.py:50
  132.4 43.5 %collective-permute-start.20 = (bf16[3,160,512]{2,1,0:T(8,128)(2,1)}, bf16[3,160,512]{2,1,0:T(8,128)(2,1)S(1)}, u32[]{:S(2)}, u32[]{:S(2)}) collective-permute-start(bf16[3,160,512]{2,1,0:T(8,128)(2,1)} %get-tuple-element.53), channel_id=1, source_target_pairs={{0,16},{4,20},{8,24},{12,28},{16,0},{20,4},{24,8},{28,12},{1,17},{... | collective-permute-start | bytes 1474568 | tf_op jit(solution)/shard_map/ppermute | solution.py:50
  135.2 19.6 %collective-permute-start.15 = (s32[2]{0:T(128)S(1)}, s32[2]{0:T(128)S(1)}, u32[]{:S(2)}, u32[]{:S(2)}) collective-permute-start(s32[2]{0:T(128)S(1)} %pad_add_fusion), channel_id=1, source_target_pairs={{0,8},{4,12},{8,0},{12,4},{16,24},{20,28},{24,16},{28,20},{1,9},{5... | collective-permute-start | bytes 32 | tf_op jit(solution)/shard_map/ppermute | solution.py:50
  155.5 3.5 %collective-permute-start.16 = (s32[4]{0:T(128)S(1)}, s32[4]{0:T(128)S(1)}, u32[]{:S(2)}, u32[]{:S(2)}) collective-permute-start(s32[4]{0:T(128)S(1)} %pad_add_fusion.1), channel_id=1, source_target_pairs={{0,16},{4,20},{8,24},{12,28},{16,0},{20,4},{24,8},{28,12},{1,17},{... | collective-permute-start | bytes 56 | tf_op jit(solution)/shard_map/ppermute | solution.py:50
  160.5 3.6 %collective-permute-start.24 = (s32[1]{0:T(128)}, s32[1]{0:T(128)}, u32[]{:S(2)}, u32[]{:S(2)}) collective-permute-start(s32[1]{0:T(128)} %bitcast.4), channel_id=1, source_target_pairs={{0,1},{1,0},{2,3},{3,2},{4,5},{5,4},{6,7},{7,6},{8,9},{9,8},{10,11... | collective-permute-start | bytes 20 | tf_op jit(solution)/shard_map/ppermute | solution.py:417
  164.6 5.4 %collective-permute-start.25 = (s32[1]{0:T(128)}, s32[1]{0:T(128)}, u32[]{:S(2)}, u32[]{:S(2)}) collective-permute-start(s32[1]{0:T(128)} %max.6), channel_id=1, source_target_pairs={{0,2},{1,3},{2,0},{3,1},{4,6},{5,7},{6,4},{7,5},{8,10},{9,11},{10,... | collective-permute-start | bytes 20 | tf_op jit(solution)/shard_map/ppermute | solution.py:417
  170.0 34.8 %collective-permute-start.21 = (bf16[3,160,512]{2,1,0:T(8,128)(2,1)}, bf16[3,160,512]{2,1,0:T(8,128)(2,1)S(1)}, u32[]{:S(2)}, u32[]{:S(2)}) collective-permute-start(bf16[3,160,512]{2,1,0:T(8,128)(2,1)} %get-tuple-element.54), channel_id=1, source_target_pairs={{0,20},{4,16},{8,28},{12,24},{16,4},{20,0},{24,12},{28,8},{1,21},{... | collective-permute-start | bytes 1474568 | tf_op jit(solution)/shard_map/ppermute | solution.py:50
  170.0 34.8 %copy-start.15 = (bf16[3,160,512]{2,1,0:T(8,128)(2,1)}, bf16[3,160,512]{2,1,0:T(8,128)(2,1)S(1)}, u32[]{:S(2)}) copy-start(bf16[3,160,512]{2,1,0:T(8,128)(2,1)S(1)} %collective-permute-done.17.refs_1_) | copy-start | bytes 1474564
  170.0 34.8 %collective-permute-start.22 = (bf16[3,160,512]{2,1,0:T(8,128)(2,1)S(1)}, bf16[3,160,512]{2,1,0:T(8,128)(2,1)S(1)}, u32[]{:S(2)}, u32[]{:S(2)}) collective-permute-start(bf16[3,160,512]{2,1,0:T(8,128)(2,1)S(1)} %copy-done.37), channel_id=1, source_target_pairs={{0,24},{4,28},{8,16},{12,20},{16,8},{20,12},{24,0},{28,4},{1,25},{... | collective-permute-start | bytes 1474568 | tf_op jit(solution)/shard_map/ppermute | solution.py:50
  172.5 32.3 %copy-start.16 = (bf16[3,160,512]{2,1,0:T(8,128)(2,1)}, bf16[3,160,512]{2,1,0:T(8,128)(2,1)S(1)}, u32[]{:S(2)}) copy-start(bf16[3,160,512]{2,1,0:T(8,128)(2,1)S(1)} %collective-permute-done.18.refs_2_) | copy-start | bytes 1474564
  172.5 32.3 %collective-permute-start.23 = (bf16[3,160,512]{2,1,0:T(8,128)(2,1)S(1)}, bf16[3,160,512]{2,1,0:T(8,128)(2,1)S(1)}, u32[]{:S(2)}, u32[]{:S(2)}) collective-permute-start(bf16[3,160,512]{2,1,0:T(8,128)(2,1)S(1)} %copy-done.36), channel_id=1, source_target_pairs={{0,28},{4,24},{8,20},{12,16},{16,12},{20,8},{24,4},{28,0},{1,29},{... | collective-permute-start | bytes 1474568 | tf_op jit(solution)/shard_map/ppermute | solution.py:50
  217.9 32.7 %copy-start = (bf16[384,512]{1,0:T(8,128)(2,1)}, bf16[384,512]{1,0:T(8,128)(2,1)S(1)}, u32[]{:S(2)}) copy-start(bf16[384,512]{1,0:T(8,128)(2,1)S(1)} %get-tuple-element.93.refs_1_) | copy-start | bytes 1179652
  217.9 32.7 %copy-start.1 = (bf16[384,512]{1,0:T(8,128)(2,1)}, bf16[384,512]{1,0:T(8,128)(2,1)S(1)}, u32[]{:S(2)}) copy-start(bf16[384,512]{1,0:T(8,128)(2,1)S(1)} %get-tuple-element.94.refs_0_) | copy-start | bytes 1179652
  218.0 2.9 collective-permute-start.26
  218.3 11.9 %collective-permute-start.28 = (bf16[384,512]{1,0:T(8,128)(2,1)S(1)}, bf16[384,512]{1,0:T(8,128)(2,1)S(1)}, u32[]{:S(2)}, u32[]{:S(2)}) collective-permute-start(bf16[384,512]{1,0:T(8,128)(2,1)S(1)} %get-tuple-element.94.refs_0_), channel_id=1, source_target_pairs={{0,8},{4,12},{8,0},{12,4},{16,24},{20,28},{24,16},{28,20},{1,9},{5... | collective-permute-start | bytes 1179656 | tf_op jit(solution)/shard_map/ppermute | solution.py:50
  219.7 10.5 %collective-permute-start.27 = (bf16[384,512]{1,0:T(8,128)(2,1)S(1)}, bf16[384,512]{1,0:T(8,128)(2,1)S(1)}, u32[]{:S(2)}, u32[]{:S(2)}) collective-permute-start(bf16[384,512]{1,0:T(8,128)(2,1)S(1)} %get-tuple-element.93.refs_1_), channel_id=1, source_target_pairs={{0,4},{4,0},{8,12},{12,8},{16,20},{20,16},{24,28},{28,24},{1,5},{5... | collective-permute-start | bytes 1179656 | tf_op jit(solution)/shard_map/ppermute | solution.py:50
  219.7 11.9 %collective-permute-start.33 = (bf16[384,512]{1,0:T(8,128)(2,1)S(1)}, bf16[384,512]{1,0:T(8,128)(2,1)S(1)}, u32[]{:S(2)}, u32[]{:S(2)}) collective-permute-start(bf16[384,512]{1,0:T(8,128)(2,1)S(1)} %get-tuple-element.93.refs_1_), channel_id=1, source_target_pairs={{0,16},{4,20},{8,24},{12,28},{16,0},{20,4},{24,8},{28,12},{1,17},{... | collective-permute-start | bytes 1179656 | tf_op jit(solution)/shard_map/ppermute | solution.py:50
  220.3 18.3 %collective-permute-start.29 = (bf16[384,512]{1,0:T(8,128)(2,1)S(1)}, bf16[384,512]{1,0:T(8,128)(2,1)S(1)}, u32[]{:S(2)}, u32[]{:S(2)}) collective-permute-start(bf16[384,512]{1,0:T(8,128)(2,1)S(1)} %get-tuple-element.93.refs_1_), channel_id=1, source_target_pairs={{0,8},{4,12},{8,0},{12,4},{16,24},{20,28},{24,16},{28,20},{1,9},{5... | collective-permute-start | bytes 1179656 | tf_op jit(solution)/shard_map/ppermute | solution.py:50
  220.9 19.2 %collective-permute-start.32 = (bf16[384,512]{1,0:T(8,128)(2,1)S(1)}, bf16[384,512]{1,0:T(8,128)(2,1)S(1)}, u32[]{:S(2)}, u32[]{:S(2)}) collective-permute-start(bf16[384,512]{1,0:T(8,128)(2,1)S(1)} %get-tuple-element.94.refs_0_), channel_id=1, source_target_pairs={{0,16},{4,20},{8,24},{12,28},{16,0},{20,4},{24,8},{28,12},{1,17},{... | collective-permute-start | bytes 1179656 | tf_op jit(solution)/shard_map/ppermute | solution.py:50
  230.2 9.9 %collective-permute-start.30 = (bf16[384,512]{1,0:T(8,128)(2,1)S(1)}, bf16[384,512]{1,0:T(8,128)(2,1)S(1)}, u32[]{:S(2)}, u32[]{:S(2)}) collective-permute-start(bf16[384,512]{1,0:T(8,128)(2,1)S(1)} %collective-permute-done.28.refs_8_), channel_id=1, source_target_pairs={{0,4},{4,0},{8,12},{12,8},{16,20},{20,16},{24,28},{28,24},{1,5},{5... | collective-permute-start | bytes 1179656 | tf_op jit(solution)/shard_map/ppermute | solution.py:50
  230.2 17.9 %collective-permute-start.36 = (bf16[384,512]{1,0:T(8,128)(2,1)S(1)}, bf16[384,512]{1,0:T(8,128)(2,1)S(1)}, u32[]{:S(2)}, u32[]{:S(2)}) collective-permute-start(bf16[384,512]{1,0:T(8,128)(2,1)S(1)} %collective-permute-done.28.refs_8_), channel_id=1, source_target_pairs={{0,16},{4,20},{8,24},{12,28},{16,0},{20,4},{24,8},{28,12},{1,17},{... | collective-permute-start | bytes 1179656 | tf_op jit(solution)/shard_map/ppermute | solution.py:50
  231.7 16.5 %collective-permute-start.37 = (bf16[384,512]{1,0:T(8,128)(2,1)S(1)}, bf16[384,512]{1,0:T(8,128)(2,1)S(1)}, u32[]{:S(2)}, u32[]{:S(2)}) collective-permute-start(bf16[384,512]{1,0:T(8,128)(2,1)S(1)} %collective-permute-done.33.refs_17_), channel_id=1, source_target_pairs={{0,8},{4,12},{8,0},{12,4},{16,24},{20,28},{24,16},{28,20},{1,9},{5... | collective-permute-start | bytes 1179656 | tf_op jit(solution)/shard_map/ppermute | solution.py:50
  238.6 10.0 %collective-permute-start.35 = (bf16[384,512]{1,0:T(8,128)(2,1)S(1)}, bf16[384,512]{1,0:T(8,128)(2,1)S(1)}, u32[]{:S(2)}, u32[]{:S(2)}) collective-permute-start(bf16[384,512]{1,0:T(8,128)(2,1)S(1)} %collective-permute-done.33.refs_17_), channel_id=1, source_target_pairs={{0,4},{4,0},{8,12},{12,8},{16,20},{20,16},{24,28},{28,24},{1,5},{5... | collective-permute-start | bytes 1179656 | tf_op jit(solution)/shard_map/ppermute | solution.py:50
  240.1 8.6 %collective-permute-start.31 = (bf16[384,512]{1,0:T(8,128)(2,1)S(1)}, bf16[384,512]{1,0:T(8,128)(2,1)S(1)}, u32[]{:S(2)}, u32[]{:S(2)}) collective-permute-start(bf16[384,512]{1,0:T(8,128)(2,1)S(1)} %collective-permute-done.29.refs_9_), channel_id=1, source_target_pairs={{0,4},{4,0},{8,12},{12,8},{16,20},{20,16},{24,28},{28,24},{1,5},{5... | collective-permute-start | bytes 1179656 | tf_op jit(solution)/shard_map/ppermute | solution.py:50
  240.1 8.5 %collective-permute-start.34 = (bf16[384,512]{1,0:T(8,128)(2,1)S(1)}, bf16[384,512]{1,0:T(8,128)(2,1)S(1)}, u32[]{:S(2)}, u32[]{:S(2)}) collective-permute-start(bf16[384,512]{1,0:T(8,128)(2,1)S(1)} %collective-permute-done.32.refs_16_), channel_id=1, source_target_pairs={{0,4},{4,0},{8,12},{12,8},{16,20},{20,16},{24,28},{28,24},{1,5},{5... | collective-permute-start | bytes 1179656 | tf_op jit(solution)/shard_map/ppermute | solution.py:50
  248.1 1.7 collective-permute-start.38
  248.1 2.5 collective-permute-start.39
  258.5 10.5 %collective-permute-start.47 = (bf16[160,256]{1,0:T(8,128)(2,1)}, bf16[160,256]{1,0:T(8,128)(2,1)S(1)}, u32[]{:S(2)}, u32[]{:S(2)}) collective-permute-start(bf16[160,256]{1,0:T(8,128)(2,1)} %get-tuple-element.84), channel_id=1, source_target_pairs={{0,4},{4,0},{8,12},{12,8},{16,20},{20,16},{24,28},{28,24},{1,5},{5... | collective-permute-start | bytes 245768 | tf_op jit(solution)/shard_map/ppermute | solution.py:50
  258.7 10.9 %collective-permute-start.48 = (bf16[160,256]{1,0:T(8,128)(2,1)}, bf16[160,256]{1,0:T(8,128)(2,1)S(1)}, u32[]{:S(2)}, u32[]{:S(2)}) collective-permute-start(bf16[160,256]{1,0:T(8,128)(2,1)} %get-tuple-element.85), channel_id=1, source_target_pairs={{0,8},{4,12},{8,0},{12,4},{16,24},{20,28},{24,16},{28,20},{1,9},{5... | collective-permute-start | bytes 245768 | tf_op jit(solution)/shard_map/ppermute | solution.py:50
  259.3 11.7 %collective-permute-start.49 = (bf16[160,256]{1,0:T(8,128)(2,1)}, bf16[160,256]{1,0:T(8,128)(2,1)S(1)}, u32[]{:S(2)}, u32[]{:S(2)}) collective-permute-start(bf16[160,256]{1,0:T(8,128)(2,1)} %get-tuple-element.86), channel_id=1, source_target_pairs={{0,12},{4,8},{8,4},{12,0},{16,28},{20,24},{24,20},{28,16},{1,13},{... | collective-permute-start | bytes 245768 | tf_op jit(solution)/shard_map/ppermute | solution.py:50
  260.4 11.9 %collective-permute-start.50 = (bf16[160,256]{1,0:T(8,128)(2,1)}, bf16[160,256]{1,0:T(8,128)(2,1)S(1)}, u32[]{:S(2)}, u32[]{:S(2)}) collective-permute-start(bf16[160,256]{1,0:T(8,128)(2,1)} %get-tuple-element.87), channel_id=1, source_target_pairs={{0,16},{4,20},{8,24},{12,28},{16,0},{20,4},{24,8},{28,12},{1,17},{... | collective-permute-start | bytes 245768 | tf_op jit(solution)/shard_map/ppermute | solution.py:50
  268.8 11.8 %collective-permute-start.40 = (bf16[160,384]{1,0:T(8,128)(2,1)}, bf16[160,384]{1,0:T(8,128)(2,1)S(1)}, u32[]{:S(2)}, u32[]{:S(2)}) collective-permute-start(bf16[160,384]{1,0:T(8,128)(2,1)} %get-tuple-element.75), channel_id=1, source_target_pairs={{0,4},{4,0},{8,12},{12,8},{16,20},{20,16},{24,28},{28,24},{1,5},{5... | collective-permute-start | bytes 368648 | tf_op jit(solution)/shard_map/ppermute | solution.py:50
  269.0 12.7 %collective-permute-start.41 = (bf16[160,384]{1,0:T(8,128)(2,1)}, bf16[160,384]{1,0:T(8,128)(2,1)S(1)}, u32[]{:S(2)}, u32[]{:S(2)}) collective-permute-start(bf16[160,384]{1,0:T(8,128)(2,1)} %get-tuple-element.76), channel_id=1, source_target_pairs={{0,8},{4,12},{8,0},{12,4},{16,24},{20,28},{24,16},{28,20},{1,9},{5... | collective-permute-start | bytes 368648 | tf_op jit(solution)/shard_map/ppermute | solution.py:50
  269.6 4.6 %collective-permute-start.51 = (bf16[160,256]{1,0:T(8,128)(2,1)S(1)}, bf16[160,256]{1,0:T(8,128)(2,1)S(1)}, u32[]{:S(2)}, u32[]{:S(2)}) collective-permute-start(bf16[160,256]{1,0:T(8,128)(2,1)S(1)} %copy-done.40), channel_id=1, source_target_pairs={{0,20},{4,16},{8,28},{12,24},{16,4},{20,0},{24,12},{28,8},{1,21},{... | collective-permute-start | bytes 245768 | tf_op jit(solution)/shard_map/ppermute | solution.py:50
  270.9 7.2 %collective-permute-start.52 = (bf16[160,256]{1,0:T(8,128)(2,1)S(1)}, bf16[160,256]{1,0:T(8,128)(2,1)S(1)}, u32[]{:S(2)}, u32[]{:S(2)}) collective-permute-start(bf16[160,256]{1,0:T(8,128)(2,1)S(1)} %copy-done.39), channel_id=1, source_target_pairs={{0,24},{4,28},{8,16},{12,20},{16,8},{20,12},{24,0},{28,4},{1,25},{... | collective-permute-start | bytes 245768 | tf_op jit(solution)/shard_map/ppermute | solution.py:50
  272.3 8.1 %collective-permute-start.53 = (bf16[160,256]{1,0:T(8,128)(2,1)S(1)}, bf16[160,256]{1,0:T(8,128)(2,1)S(1)}, u32[]{:S(2)}, u32[]{:S(2)}) collective-permute-start(bf16[160,256]{1,0:T(8,128)(2,1)S(1)} %copy-done.38), channel_id=1, source_target_pairs={{0,28},{4,24},{8,20},{12,16},{16,12},{20,8},{24,4},{28,0},{1,29},{... | collective-permute-start | bytes 245768 | tf_op jit(solution)/shard_map/ppermute | solution.py:50
  274.1 8.8 %collective-permute-start.42 = (bf16[160,384]{1,0:T(8,128)(2,1)}, bf16[160,384]{1,0:T(8,128)(2,1)S(1)}, u32[]{:S(2)}, u32[]{:S(2)}) collective-permute-start(bf16[160,384]{1,0:T(8,128)(2,1)} %get-tuple-element.77), channel_id=1, source_target_pairs={{0,12},{4,8},{8,4},{12,0},{16,28},{20,24},{24,20},{28,16},{1,13},{... | collective-permute-start | bytes 368648 | tf_op jit(solution)/shard_map/ppermute | solution.py:50
  278.2 11.9 %collective-permute-start.43 = (bf16[160,384]{1,0:T(8,128)(2,1)}, bf16[160,384]{1,0:T(8,128)(2,1)S(1)}, u32[]{:S(2)}, u32[]{:S(2)}) collective-permute-start(bf16[160,384]{1,0:T(8,128)(2,1)} %get-tuple-element.78), channel_id=1, source_target_pairs={{0,16},{4,20},{8,24},{12,28},{16,0},{20,4},{24,8},{28,12},{1,17},{... | collective-permute-start | bytes 368648 | tf_op jit(solution)/shard_map/ppermute | solution.py:50
  280.5 11.7 %collective-permute-start.44 = (bf16[160,384]{1,0:T(8,128)(2,1)}, bf16[160,384]{1,0:T(8,128)(2,1)S(1)}, u32[]{:S(2)}, u32[]{:S(2)}) collective-permute-start(bf16[160,384]{1,0:T(8,128)(2,1)} %get-tuple-element.79), channel_id=1, source_target_pairs={{0,20},{4,16},{8,28},{12,24},{16,4},{20,0},{24,12},{28,8},{1,21},{... | collective-permute-start | bytes 368648 | tf_op jit(solution)/shard_map/ppermute | solution.py:50
  280.6 11.6 %collective-permute-start.45 = (bf16[160,384]{1,0:T(8,128)(2,1)}, bf16[160,384]{1,0:T(8,128)(2,1)S(1)}, u32[]{:S(2)}, u32[]{:S(2)}) collective-permute-start(bf16[160,384]{1,0:T(8,128)(2,1)} %get-tuple-element.80), channel_id=1, source_target_pairs={{0,24},{4,28},{8,16},{12,20},{16,8},{20,12},{24,0},{28,4},{1,25},{... | collective-permute-start | bytes 368648 | tf_op jit(solution)/shard_map/ppermute | solution.py:50
  281.7 10.4 %collective-permute-start.46 = (bf16[160,384]{1,0:T(8,128)(2,1)}, bf16[160,384]{1,0:T(8,128)(2,1)S(1)}, u32[]{:S(2)}, u32[]{:S(2)}) collective-permute-start(bf16[160,384]{1,0:T(8,128)(2,1)} %get-tuple-element.81), channel_id=1, source_target_pairs={{0,28},{4,24},{8,20},{12,16},{16,12},{20,8},{24,4},{28,0},{1,29},{... | collective-permute-start | bytes 368648 | tf_op jit(solution)/shard_map/ppermute | solution.py:50
  (35 other events, 387.8 us)
Sparse Core Ops, SparseCore 0:
  128.5 48.6 all-gather.4
  178.8 62.2 all-gather.2

commit v4 on v3

--- a/solution.py
+++ b/solution.py
@@ -11,13 +11,12 @@
 BLOCK = 32
 SENTINEL = 32.0
 LIMIT = 24.0
-VMEM = 56 * 1024 * 1024
 QUERY_TILE = 256
 UNIT = 128
 
 
-def params(limit=VMEM):
-    return pltpu.CompilerParams(vmem_limit_bytes=limit)
+def params(mebibytes):
+    return pltpu.CompilerParams(vmem_limit_bytes=mebibytes * 1024 * 1024)
 
 
 def order(count):
@@ -57,41 +56,49 @@
     columns = out_weight.shape[1] // count
     slicing = all(size % HEAD_DIM == 0 for size in sizes)
     chunks = len(sizes) if slicing else 0
+    staged = columns if slicing else HEAD_DIM
 
     def body(place_ref, blocks_ref, mask_ref, q_ref, k_ref, v_ref, w_ref, *refs):
         out_refs = refs[:count]
         weight_refs = refs[count : count + chunks]
-        key_in, key_out, key_sem, sems, weight_sems = refs[count + chunks :]
-        load = pltpu.make_async_copy(k_ref.at[0], key_in, key_sem.at[0])
-        load.start()
+        held, key_out, w_held, load_sems, sems, weight_sems = refs[count + chunks :]
+        loads = []
+        for slot, ref in enumerate((k_ref, q_ref, v_ref)):
+            load = pltpu.make_async_copy(ref.at[0], held.at[slot], load_sems.at[slot])
+            load.start()
+            loads.append(load)
+        if chunks:
+            start = pl.multiple_of(place_ref[0] * columns, HEAD_DIM)
+            load = pltpu.make_async_copy(
+                w_ref.at[:, pl.ds(start, columns)], w_held, load_sems.at[3]
+            )
+            load.start()
+            loads.append(load)
+        starts = [pl.multiple_of((place_ref[0] ^ m) * width, HEAD_DIM) for m in range(count)]
+        good = valid_column(mask_ref, blocks_ref[0, 0]) > 0.5
         copies = []
-        for index in range(chunks):
-            start = pl.multiple_of(place_ref[0] * columns + sum(sizes[:index]), HEAD_DIM)
-            copy = pltpu.make_async_copy(
-                w_ref.at[:, pl.ds(start, sizes[index])],
-                weight_refs[index],
-                weight_sems.at[index],
-            )
+
+        def send(source, target, sem):
+            copy = pltpu.make_async_copy(source, target, sem)
             copy.start()
             copies.append(copy)
-        starts = [pl.multiple_of((place_ref[0] ^ m) * width, HEAD_DIM) for m in range(count)]
+
+        loads[0].wait()
         for mask in range(count):
-            for slot, ref in ((0, q_ref), (2, v_ref)):
-                copy = pltpu.make_async_copy(
-                    ref.at[0, :, pl.ds(starts[mask], width)],
-                    out_refs[mask].at[slot],
-                    sems.at[mask, slot],
-                )
-                copy.start()
-                copies.append(copy)
-        good = valid_column(mask_ref, blocks_ref[0, 0]) > 0.5
-        load.wait()
-        for mask in range(count):
-            part = key_in[:, pl.ds(starts[mask], width)]
+            part = held[0, :, pl.ds(starts[mask], width)]
             key_out[mask] = jnp.where(good, part, jnp.bfloat16(SENTINEL))
-            copy = pltpu.make_async_copy(key_out.at[mask], out_refs[mask].at[1], sems.at[mask, 1])
-            copy.start()
-            copies.append(copy)
+            send(key_out.at[mask], out_refs[mask].at[1], sems.at[mask, 1])
+        for slot, target in ((1, 0), (2, 2)):
+            loads[slot].wait()
+            for mask in range(count):
+                source = held.at[slot, :, pl.ds(starts[mask], width)]
+                send(source, out_refs[mask].at[target], sems.at[mask, target])
+        if chunks:
+            loads[3].wait()
+            for index in range(chunks):
+                first = sum(sizes[:index])
+                source = w_held.at[:, first : first + sizes[index]]
+                send(source, weight_refs[index], weight_sems.at[index])
         for copy in copies:
             copy.wait()
 
@@ -107,15 +114,16 @@
             in_specs=[full_spec((1, rows))] + [any_spec] * 4,
             out_specs=[any_spec] * (count + chunks),
             scratch_shapes=[
-                pltpu.VMEM((rows, features), jnp.bfloat16),
+                pltpu.VMEM((3, rows, features), jnp.bfloat16),
                 pltpu.VMEM((count, rows, width), jnp.bfloat16),
-                pltpu.SemaphoreType.DMA((1,)),
+                pltpu.VMEM((depth, staged), jnp.bfloat16),
+                pltpu.SemaphoreType.DMA((4,)),
                 pltpu.SemaphoreType.DMA((count, 3)),
                 pltpu.SemaphoreType.DMA((len(sizes),)),
             ],
         ),
         out_shape=[jax.ShapeDtypeStruct((3, rows, width), jnp.bfloat16)] * count + weight_shapes,
-        compiler_params=params(),
+        compiler_params=params(56),
         cost_estimate=pl.CostEstimate(
             flops=0, bytes_accessed=12 * rows * features, transcendentals=0
         ),
@@ -146,21 +154,28 @@
     return pl.ds(start if isinstance(start, int) else pl.multiple_of(start, BLOCK), size)
 
 
-def attend(place, counts, received, rows):
+def attend(place, received, rows):
     count = len(received)
     width = received[0].shape[2]
     total = count * rows
     factor = math.log2(math.e) / math.sqrt(HEAD_DIM)
 
-    def body(place_ref, counts_ref, *refs):
+    def body(place_ref, *refs):
         parts = refs[:count]
-        out_ref = refs[count]
-        query_all, key_all, value_all, value_t, result, table = refs[count + 1 :]
-        by_mask, by_view, used = packed_offsets(place_ref, counts_ref, table, count)
+        out_ref, counts_ref = refs[count : count + 2]
+        query_all, key_all, value_all, value_t, result, table = refs[count + 2 :]
 
         @pl.when(pl.program_id(0) == 0)
         def _():
             value_all[...] = jnp.zeros_like(value_all)
+            for mask in range(count):
+                blocks = jnp.zeros((1, HEAD_DIM), jnp.float32)
+                for first in range(0, rows, BLOCK):
+                    row = parts[mask][1, first : first + 16, :].astype(jnp.float32)[:1]
+                    blocks = blocks + jnp.where(row < LIMIT, 1.0, 0.0)
+                counts_ref[mask] = jnp.max(blocks).astype(jnp.int32)
+
+        by_mask, by_view, used = packed_offsets(place_ref, counts_ref, table, count)
 
         for mask in range(count):
             where = rows_at(by_mask[mask], rows)
@@ -211,10 +226,13 @@
     return pl.pallas_call(
         body,
         grid_spec=pltpu.PrefetchScalarGridSpec(
-            num_scalar_prefetch=2,
+            num_scalar_prefetch=1,
             grid=(width // HEAD_DIM,),
             in_specs=[pl.BlockSpec((3, rows, HEAD_DIM), lambda h, *_: (0, 0, h))] * count,
-            out_specs=pl.BlockSpec((total, HEAD_DIM), lambda h, *_: (0, h)),
+            out_specs=[
+                pl.BlockSpec((total, HEAD_DIM), lambda h, *_: (0, h)),
+                pl.BlockSpec(memory_space=pltpu.SMEM),
+            ],
             scratch_shapes=[
                 pltpu.VMEM((total, HEAD_DIM), jnp.bfloat16),
                 pltpu.VMEM((total + total // 5, HEAD_DIM), jnp.bfloat16),
@@ -224,13 +242,16 @@
                 pltpu.SMEM((count,), jnp.int32),
             ],
         ),
-        out_shape=jax.ShapeDtypeStruct((total, width), jnp.bfloat16),
-        compiler_params=params(),
+        out_shape=[
+            jax.ShapeDtypeStruct((total, width), jnp.bfloat16),
+            jax.ShapeDtypeStruct((count,), jnp.int32),
+        ],
+        compiler_params=params(24),
         cost_estimate=pl.CostEstimate(
             flops=flops, bytes_accessed=8 * total * width, transcendentals=flops // 512
         ),
         name="attend",
-    )(place, counts, *received)
+    )(place, *received)
 
 
 def gather_features(own, count):
@@ -352,7 +373,7 @@
             ],
         ),
         out_shape=[jax.ShapeDtypeStruct((rows, columns), jnp.bfloat16)] * count,
-        compiler_params=params(),
+        compiler_params=params(36),
         cost_estimate=pl.CostEstimate(
             flops=total * count * width * columns,
             bytes_accessed=total * count * width,
@@ -395,7 +416,7 @@
             out_specs=full_spec((rows, count * columns)),
         ),
         out_shape=jax.ShapeDtypeStruct((rows, count * columns), jnp.bfloat16),
-        compiler_params=params(),
+        compiler_params=params(16),
         cost_estimate=pl.CostEstimate(
             flops=0, bytes_accessed=4 * rows * count * columns, transcendentals=0
         ),
@@ -403,20 +424,14 @@
     )(place, block_counts, row_mask, *[piece for chunk in chunks for piece in chunk])
 
 
-def share_counts(block_counts, count):
-    counts = block_counts[0]
-    step = 1
-    while step < count:
-        counts = jnp.concatenate([counts, xor_permute(counts, step, count)])
-        step *= 2
-    most = jnp.sum(counts)[None]
+def largest(value):
     groups = lax.axis_size("fsdp")
     step = 1
     while step < groups:
         pairs = [(group, group ^ step) for group in range(groups)]
-        most = jnp.maximum(most, lax.ppermute(most, "fsdp", pairs))
+        value = jnp.maximum(value, lax.ppermute(value, "fsdp", pairs))
         step *= 2
-    return counts, most[0]
+    return value
 
 
 def local(queries, keys, values, out_weight, block_counts, row_mask):
@@ -425,8 +440,7 @@
     total = count * rows
     place_array = jnp.full((1,), lax.axis_index("cam"), jnp.int32)
     columns = out_weight.shape[1] // count
-    first = max(HEAD_DIM, -(-columns * 3 // 5 // HEAD_DIM) * HEAD_DIM)
-    sizes = [first, columns - first]
+    sizes = [columns - columns // 5, columns // 5]
 
     payloads, weights = pack(
         place_array, block_counts, row_mask, queries, keys, values, out_weight, sizes, count
@@ -435,12 +449,13 @@
     received = [payloads[0]] + [None] * (count - 1)
     for mask in order(count):
         received[mask] = xor_permute(payloads[mask], mask, count)
-    counts, most = share_counts(block_counts, count)
-    attended = attend(place_array, counts, received, rows)
+    attended, counts = attend(place_array, received, rows)
+    most = largest(jnp.sum(counts)[None])[0]
 
     always = total * 3 // 5
     features = gather_features(attended[:always], count)
     rest = attended[always:]
+    features, rest = lax.optimization_barrier((features, rest))
     shapes = [jax.ShapeDtypeStruct((rest.shape[0] // 2, rest.shape[1]), rest.dtype)] * 2 * count
     more = lax.cond(
         most * BLOCK > always,

time: 302 us -> 187 us (0.62)
  the two profiles are of different devices: /device:TPU:0 before, /device:TPU:9 now
where the time goes in v4:
time: 187 us
  waiting for transfers between devices  65.4 us (35%)
  Pallas kernels  38.7 us (21%)
  starting transfers between devices  38.6 us (21%)
  local copies, waits for them, and re-layouts  27.9 us (15%)
  between operations  16.1 us (9%)
    ppermute x35, waiting for transfers between devices, xor_permute(): lax.ppermute(array, 'cam', [(place, place ^ mask) for place in range(coun...  61.7 us
    ppermute x35, starting transfers between devices, xor_permute(): lax.ppermute(array, 'cam', [(place, place ^ mask) for place in range(coun...  34 us
    unnamed x76, local copies, waits for them, and re-layouts  26 us
    pallas_call x2, Pallas kernels, project(): pl.pallas_call(body, grid_spec=pltpu.PrefetchScalarGridSpec(num_scalar_pr...  19.1 us
    pallas_call x1, Pallas kernels, attend(): pl.pallas_call(body, grid_spec=pltpu.PrefetchScalarGridSpec(num_scalar_pr...  12 us
    pallas_call x1, Pallas kernels, pack(): pl.pallas_call(body, grid_spec=pltpu.PrefetchScalarGridSpec(num_scalar_pr...  5.07 us
    ppermute x2, starting transfers between devices, largest(): value = jnp.maximum(value, lax.ppermute(value, 'fsdp', pairs))  4.55 us
  transfers between devices with their start and end apart: 39, of which 13 were waited for; matrix products, arithmetic and copies ran while one was open for 1% of the time, Pallas kernels for 17%

profile of v4, /device:TPU:9, one launch (start us, length us, event | category | flops | bytes accessed | tf_op | source)
XLA Modules:
  0.0 187.4 jit_solution(7776707338322253206)
XLA Ops:
  7.2 5.1 %pack.1 = (bf16[3,160,512]{2,1,0:T(8,128)(2,1)}, bf16[3,160,512]{2,1,0:T(8,128)(2,1)}, bf16[3,160,512]{2,1,0:T(8,128)(2,1)}, bf16[3,160,512]{2,1,0:T(8,128)(2,1)...) custom-call(s32[1]{0:T(128)} %bitcast.place_ref, ...), custom_call_target="tpu_custom_call" | custom-call | bytes 7864320 | tf_op jit(solution)/shard_map/pack/pallas_call | solution.py:109
  13.1 1.2 collective-permute-start.15
  14.8 1.2 collective-permute-start.17
  16.6 2.2 %collective-permute-start.19 = (bf16[3,160,512]{2,1,0:T(8,128)(2,1)}, bf16[3,160,512]{2,1,0:T(8,128)(2,1)}, u32[]{:S(2)}, u32[]{:S(2)}) collective-permute-start(bf16[3,160,512]{2,1,0:T(8,128)(2,1)} %get-tuple-element.73), channel_id=1, source_target_pairs={{0,24},{4,28},{8,16},{12,20},{16,8},{20,12},{24,0},{28,4},{1,25},{... | collective-permute-start | bytes 1474568 | tf_op jit(solution)/shard_map/ppermute | solution.py:49
  18.8 7.3 %collective-permute-done.15.refs_2_ = bf16[3,160,512]{2,1,0:T(8,128)(2,1)S(1)} collective-permute-done((bf16[3,160,512]{2,1,0:T(8,128)(2,1)}, bf16[3,160,512]{2,1,0:T(8,128)(2,1)S(1)}, u32[]{:S(2)}, u32[]{:S(2)}) %collective-permute-start.15) | collective-permute-done | bytes 491552 | tf_op jit(solution)/shard_map/ppermute | solution.py:49
  26.1 3.4 %collective-permute-start.20 = (bf16[3,160,512]{2,1,0:T(8,128)(2,1)}, bf16[3,160,512]{2,1,0:T(8,128)(2,1)}, u32[]{:S(2)}, u32[]{:S(2)}) collective-permute-start(bf16[3,160,512]{2,1,0:T(8,128)(2,1)} %get-tuple-element.74), channel_id=1, source_target_pairs={{0,28},{4,24},{8,20},{12,16},{16,12},{20,8},{24,4},{28,0},{1,29},{... | collective-permute-start | bytes 1474568 | tf_op jit(solution)/shard_map/ppermute | solution.py:49
  29.5 8.2 %collective-permute-done.16.refs_3_ = bf16[3,160,512]{2,1,0:T(8,128)(2,1)S(1)} collective-permute-done((bf16[3,160,512]{2,1,0:T(8,128)(2,1)}, bf16[3,160,512]{2,1,0:T(8,128)(2,1)S(1)}, u32[]{:S(2)}, u32[]{:S(2)}) %collective-permute-start.16) | collective-permute-done | bytes 491552 | tf_op jit(solution)/shard_map/ppermute | solution.py:49
  37.7 21.9 %collective-permute-done.18.refs_5_ = bf16[3,160,512]{2,1,0:T(8,128)(2,1)S(1)} collective-permute-done((bf16[3,160,512]{2,1,0:T(8,128)(2,1)}, bf16[3,160,512]{2,1,0:T(8,128)(2,1)S(1)}, u32[]{:S(2)}, u32[]{:S(2)}) %collective-permute-start.18) | collective-permute-done | bytes 491552 | tf_op jit(solution)/shard_map/ppermute | solution.py:49
  59.6 12.0 %attend.1 = (bf16[1280,512]{1,0:T(8,128)(2,1)S(1)}, s32[8]{0:T(128)S(1)}) custom-call(s32[1]{0:T(128)} %bitcast.place_ref, bf16[3,160,512]{2,1,0:T(8,128)(2,1)S(1)} %copy-done.24, bf16[3,160,512]{2,1,0:T(8,128)(2,1)S(1)} %collective-permute-done.14.refs_1_, bf16[3,160,512]{2,1,0:T(8,128)(2,1)S(1)} %collective-permute-done.15.refs_2_, ...), custom_call_target="tpu_custom_call" | custom-call | flops 838860800 | bytes 5242880 | tf_op jit(solution)/shard_map/attend/pallas_call | solution.py:226
  71.7 1.3 collective-permute-start.23
  72.9 1.2 collective-permute-start.28
  75.8 3.0 %collective-permute-done.35 = s32[1]{0:T(128)} collective-permute-done((s32[1]{0:T(128)}, s32[1]{0:T(128)}, u32[]{:S(2)}, u32[]{:S(2)}) %collective-permute-start.35) | collective-permute-done | bytes 36 | tf_op jit(solution)/shard_map/ppermute | solution.py:432
  80.0 4.5 %collective-permute-start.36 = (s32[1]{0:T(128)}, s32[1]{0:T(128)}, u32[]{:S(2)}, u32[]{:S(2)}) collective-permute-start(s32[1]{0:T(128)} %max.6), channel_id=1, source_target_pairs={{0,2},{1,3},{2,0},{3,1},{4,6},{5,7},{6,4},{7,5},{8,10},{9,11},{10,... | collective-permute-start | bytes 20 | tf_op jit(solution)/shard_map/ppermute | solution.py:432
  86.1 1.3 collective-permute-start.31
  87.3 3.5 %collective-permute-done.24.refs_9_ = bf16[384,512]{1,0:T(8,128)(2,1)S(1)} collective-permute-done((bf16[384,512]{1,0:T(8,128)(2,1)S(1)}, bf16[384,512]{1,0:T(8,128)(2,1)S(1)}, u32[]{:S(2)}, u32[]{:S(2)}) %collective-permute-start.24) | collective-permute-done | bytes 393248 | tf_op jit(solution)/shard_map/ppermute | solution.py:49
  90.8 1.2 collective-permute-start.32
  92.1 1.7 collective-permute-start.25
  94.3 5.8 %collective-permute-done.31.refs_24_ = bf16[384,512]{1,0:T(8,128)(2,1)S(1)} collective-permute-done((bf16[384,512]{1,0:T(8,128)(2,1)S(1)}, bf16[384,512]{1,0:T(8,128)(2,1)S(1)}, u32[]{:S(2)}, u32[]{:S(2)}) %collective-permute-start.31) | collective-permute-done | bytes 393248 | tf_op jit(solution)/shard_map/ppermute | solution.py:49
  100.1 1.3 collective-permute-start.29
  101.3 1.0 collective-permute-start.33
  103.2 1.9 %slice.20 = bf16[512,512]{1,0:T(8,128)(2,1)} slice(bf16[1280,512]{1,0:T(8,128)(2,1)} %copy-done.22), slice={[768:1280], [0:512]} | slice | bytes 1048576 | tf_op jit(solution)/shard_map/slice | solution.py:457
  109.5 2.2 %copy-done = bf16[4096,512]{1,0:T(8,128)(2,1)S(1)} copy-done((bf16[4096,512]{1,0:T(8,128)(2,1)S(1)}, bf16[4096,512]{1,0:T(8,128)(2,1)}, u32[]{:S(2)}) %copy-start) | copy-done | bytes 4194328
  111.7 1.0 copy-done.2
  112.7 1.0 copy-done.5
  113.7 1.0 copy-done.8
  114.7 1.0 copy-done.11
  115.7 1.0 copy-done.14
  116.7 1.0 copy-done.17
  117.7 1.0 copy-done.20
  118.7 9.4 %project.2 = (bf16[160,512]{1,0:T(8,128)(2,1)S(1)}, bf16[160,512]{1,0:T(8,128)(2,1)}, bf16[160,512]{1,0:T(8,128)(2,1)}, bf16[160,512]{1,0:T(8,128)(2,1)S(1)}, bf...) custom-call(s32[1]{0:T(128)} %bitcast.place_ref, ...), custom_call_target="tpu_custom_call" | custom-call | flops 2684354560 | bytes 5242880 | tf_op jit(solution)/shard_map/project/pallas_call | solution.py:360
  132.5 1.2 collective-permute-start.38
  133.8 1.0 copy-done.3
  134.8 1.0 copy-done.6
  135.8 1.0 copy-done.9
  136.8 1.0 copy-done.12
  137.8 1.0 copy-done.15
  138.8 1.0 copy-done.18
  140.7 1.2 copy-done.23
  142.0 9.8 %project.3 = (bf16[160,128]{1,0:T(8,128)(2,1)S(1)}, bf16[160,128]{1,0:T(8,128)(2,1)S(1)}, bf16[160,128]{1,0:T(8,128)(2,1)S(1)}, bf16[160,128]{1,0:T(8,128)(2,1)S...) custom-call(s32[1]{0:T(128)} %bitcast.place_ref, ...), custom_call_target="tpu_custom_call" | custom-call | flops 671088640 | bytes 5242880 | tf_op jit(solution)/shard_map/project/pallas_call | solution.py:360
  152.4 1.6 collective-permute-start.46
  154.0 1.2 collective-permute-start.47
  155.2 2.6 %collective-permute-start.48 = (bf16[160,128]{1,0:T(8,128)(2,1)S(1)}, bf16[160,128]{1,0:T(8,128)(2,1)S(1)}, u32[]{:S(2)}, u32[]{:S(2)}) collective-permute-start(bf16[160,128]{1,0:T(8,128)(2,1)S(1)} %get-tuple-element.125), channel_id=1, source_target_pairs={{0,20},{4,16},{8,28},{12,24},{16,4},{20,0},{24,12},{28,8},{1,21},{... | collective-permute-start | bytes 122888 | tf_op jit(solution)/shard_map/ppermute | solution.py:49
  160.5 1.1 collective-permute-done.49.refs_14_
  161.9 1.3 collective-permute-done.50.refs_15_
  163.5 2.1 %collective-permute-start.42 = (bf16[160,512]{1,0:T(8,128)(2,1)S(1)}, bf16[160,512]{1,0:T(8,128)(2,1)S(1)}, u32[]{:S(2)}, u32[]{:S(2)}) collective-permute-start(bf16[160,512]{1,0:T(8,128)(2,1)S(1)} %copy-done.31), channel_id=1, source_target_pairs={{0,24},{4,28},{8,16},{12,20},{16,8},{20,12},{24,0},{28,4},{1,25},{... | collective-permute-start | bytes 491528 | tf_op jit(solution)/shard_map/ppermute | solution.py:49
  166.7 7.6 %collective-permute-done.40.refs_4_ = bf16[160,512]{1,0:T(8,128)(2,1)S(1)} collective-permute-done((bf16[160,512]{1,0:T(8,128)(2,1)S(1)}, bf16[160,512]{1,0:T(8,128)(2,1)S(1)}, u32[]{:S(2)}, u32[]{:S(2)}) %collective-permute-start.40) | collective-permute-done | bytes 163872 | tf_op jit(solution)/shard_map/ppermute | solution.py:49
  174.4 3.7 %collective-permute-done.41.refs_5_ = bf16[160,512]{1,0:T(8,128)(2,1)S(1)} collective-permute-done((bf16[160,512]{1,0:T(8,128)(2,1)S(1)}, bf16[160,512]{1,0:T(8,128)(2,1)S(1)}, u32[]{:S(2)}, u32[]{:S(2)}) %collective-permute-start.41) | collective-permute-done | bytes 163872 | tf_op jit(solution)/shard_map/ppermute | solution.py:49
  178.1 2.5 %assemble.1 = bf16[160,5120]{1,0:T(8,128)(2,1)} custom-call(s32[1]{0:T(128)} %bitcast.place_ref, s32[1,1]{1,0:T(1,128)S(6)} %copy.39.blocks_ref, s32[1,160]{1,0:T(1,128)S(1)} %copy-done.27, bf16[160,512]{1,0:T(8,128)(2,1)S(1)} %copy-done.26, bf16[160,512]{1,0:T(8,128)(2,1)} %collective-permute-done.37.refs_1_, ...), custom_call_target="tpu_custom_call" | custom-call | bytes 3276800 | tf_op jit(solution)/shard_map/assemble/pallas_call | solution.py:409
  (118 shorter events, 20.8 us)
Async XLA Ops:
  6.5 103.0 %all-gather.3.cloned.1.call-start = ((), (), s32[]{:S(2)}) async-start(), calls=%async_computation | async-start | bytes 5242880 | tf_op jit(solution)/shard_map/all_gather | solution.py:448
  12.3 47.3 %copy-start.24 = (bf16[3,160,512]{2,1,0:T(8,128)(2,1)S(1)}, bf16[3,160,512]{2,1,0:T(8,128)(2,1)}, u32[]{:S(2)}) copy-start(bf16[3,160,512]{2,1,0:T(8,128)(2,1)} %get-tuple-element.67.refs_0_) | copy-start | bytes 1474564
  12.3 121.5 %all-gather.5.cloned.1.call-start = ((), (), s32[]{:S(2)}) async-start(), calls=%async_computation.1 | async-start | bytes 1310720 | tf_op jit(solution)/shard_map/all_gather | solution.py:448
  12.4 4.3 %collective-permute-start.14 = (bf16[3,160,512]{2,1,0:T(8,128)(2,1)}, bf16[3,160,512]{2,1,0:T(8,128)(2,1)S(1)}, u32[]{:S(2)}, u32[]{:S(2)}) collective-permute-start(bf16[3,160,512]{2,1,0:T(8,128)(2,1)} %get-tuple-element.68), channel_id=1, source_target_pairs={{0,4},{4,0},{8,12},{12,8},{16,20},{20,16},{24,28},{28,24},{1,5},{5... | collective-permute-start | bytes 1474568 | tf_op jit(solution)/shard_map/ppermute | solution.py:49
  13.1 13.0 %collective-permute-start.15 = (bf16[3,160,512]{2,1,0:T(8,128)(2,1)}, bf16[3,160,512]{2,1,0:T(8,128)(2,1)S(1)}, u32[]{:S(2)}, u32[]{:S(2)}) collective-permute-start(bf16[3,160,512]{2,1,0:T(8,128)(2,1)} %get-tuple-element.69), channel_id=1, source_target_pairs={{0,8},{4,12},{8,0},{12,4},{16,24},{20,28},{24,16},{28,20},{1,9},{5... | collective-permute-start | bytes 1474568 | tf_op jit(solution)/shard_map/ppermute | solution.py:49
  14.3 23.3 %collective-permute-start.16 = (bf16[3,160,512]{2,1,0:T(8,128)(2,1)}, bf16[3,160,512]{2,1,0:T(8,128)(2,1)S(1)}, u32[]{:S(2)}, u32[]{:S(2)}) collective-permute-start(bf16[3,160,512]{2,1,0:T(8,128)(2,1)} %get-tuple-element.70), channel_id=1, source_target_pairs={{0,12},{4,8},{8,4},{12,0},{16,28},{20,24},{24,20},{28,16},{1,13},{... | collective-permute-start | bytes 1474568 | tf_op jit(solution)/shard_map/ppermute | solution.py:49
  14.8 22.8 %collective-permute-start.17 = (bf16[3,160,512]{2,1,0:T(8,128)(2,1)}, bf16[3,160,512]{2,1,0:T(8,128)(2,1)S(1)}, u32[]{:S(2)}, u32[]{:S(2)}) collective-permute-start(bf16[3,160,512]{2,1,0:T(8,128)(2,1)} %get-tuple-element.71), channel_id=1, source_target_pairs={{0,16},{4,20},{8,24},{12,28},{16,0},{20,4},{24,8},{28,12},{1,17},{... | collective-permute-start | bytes 1474568 | tf_op jit(solution)/shard_map/ppermute | solution.py:49
  16.0 43.5 %collective-permute-start.18 = (bf16[3,160,512]{2,1,0:T(8,128)(2,1)}, bf16[3,160,512]{2,1,0:T(8,128)(2,1)S(1)}, u32[]{:S(2)}, u32[]{:S(2)}) collective-permute-start(bf16[3,160,512]{2,1,0:T(8,128)(2,1)} %get-tuple-element.72), channel_id=1, source_target_pairs={{0,20},{4,16},{8,28},{12,24},{16,4},{20,0},{24,12},{28,8},{1,21},{... | collective-permute-start | bytes 1474568 | tf_op jit(solution)/shard_map/ppermute | solution.py:49
  16.6 43.0 %collective-permute-start.19 = (bf16[3,160,512]{2,1,0:T(8,128)(2,1)}, bf16[3,160,512]{2,1,0:T(8,128)(2,1)}, u32[]{:S(2)}, u32[]{:S(2)}) collective-permute-start(bf16[3,160,512]{2,1,0:T(8,128)(2,1)} %get-tuple-element.73), channel_id=1, source_target_pairs={{0,24},{4,28},{8,16},{12,20},{16,8},{20,12},{24,0},{28,4},{1,25},{... | collective-permute-start | bytes 1474568 | tf_op jit(solution)/shard_map/ppermute | solution.py:49
  26.1 33.5 %collective-permute-start.20 = (bf16[3,160,512]{2,1,0:T(8,128)(2,1)}, bf16[3,160,512]{2,1,0:T(8,128)(2,1)}, u32[]{:S(2)}, u32[]{:S(2)}) collective-permute-start(bf16[3,160,512]{2,1,0:T(8,128)(2,1)} %get-tuple-element.74), channel_id=1, source_target_pairs={{0,28},{4,24},{8,20},{12,16},{16,12},{20,8},{24,4},{28,0},{1,29},{... | collective-permute-start | bytes 1474568 | tf_op jit(solution)/shard_map/ppermute | solution.py:49
  71.7 14.4 %collective-permute-start.23 = (bf16[384,512]{1,0:T(8,128)(2,1)S(1)}, bf16[384,512]{1,0:T(8,128)(2,1)S(1)}, u32[]{:S(2)}, u32[]{:S(2)}) collective-permute-start(bf16[384,512]{1,0:T(8,128)(2,1)S(1)} %get-tuple-element.77.refs_0_), channel_id=1, source_target_pairs={{0,8},{4,12},{8,0},{12,4},{16,24},{20,28},{24,16},{28,20},{1,9},{5... | collective-permute-start | bytes 1179656 | tf_op jit(solution)/shard_map/ppermute | solution.py:49
  72.9 13.1 %collective-permute-start.28 = (bf16[384,512]{1,0:T(8,128)(2,1)S(1)}, bf16[384,512]{1,0:T(8,128)(2,1)S(1)}, u32[]{:S(2)}, u32[]{:S(2)}) collective-permute-start(bf16[384,512]{1,0:T(8,128)(2,1)S(1)} %get-tuple-element.78.refs_1_), channel_id=1, source_target_pairs={{0,16},{4,20},{8,24},{12,28},{16,0},{20,4},{24,8},{28,12},{1,17},{... | collective-permute-start | bytes 1179656 | tf_op jit(solution)/shard_map/ppermute | solution.py:49
  74.2 16.7 %collective-permute-start.24 = (bf16[384,512]{1,0:T(8,128)(2,1)S(1)}, bf16[384,512]{1,0:T(8,128)(2,1)S(1)}, u32[]{:S(2)}, u32[]{:S(2)}) collective-permute-start(bf16[384,512]{1,0:T(8,128)(2,1)S(1)} %get-tuple-element.78.refs_1_), channel_id=1, source_target_pairs={{0,8},{4,12},{8,0},{12,4},{16,24},{20,28},{24,16},{28,20},{1,9},{5... | collective-permute-start | bytes 1179656 | tf_op jit(solution)/shard_map/ppermute | solution.py:49
  74.5 17.6 %collective-permute-start.27 = (bf16[384,512]{1,0:T(8,128)(2,1)S(1)}, bf16[384,512]{1,0:T(8,128)(2,1)S(1)}, u32[]{:S(2)}, u32[]{:S(2)}) collective-permute-start(bf16[384,512]{1,0:T(8,128)(2,1)S(1)} %get-tuple-element.77.refs_0_), channel_id=1, source_target_pairs={{0,16},{4,20},{8,24},{12,28},{16,0},{20,4},{24,8},{28,12},{1,17},{... | collective-permute-start | bytes 1179656 | tf_op jit(solution)/shard_map/ppermute | solution.py:49
  75.8 3.0 %collective-permute-start.35 = (s32[1]{0:T(128)}, s32[1]{0:T(128)}, u32[]{:S(2)}, u32[]{:S(2)}) collective-permute-start(s32[1]{0:T(128)} %bitcast.1), channel_id=1, source_target_pairs={{0,1},{1,0},{2,3},{3,2},{4,5},{5,4},{6,7},{7,6},{8,9},{9,8},{10,11... | collective-permute-start | bytes 20 | tf_op jit(solution)/shard_map/ppermute | solution.py:432
  80.0 5.2 %collective-permute-start.36 = (s32[1]{0:T(128)}, s32[1]{0:T(128)}, u32[]{:S(2)}, u32[]{:S(2)}) collective-permute-start(s32[1]{0:T(128)} %max.6), channel_id=1, source_target_pairs={{0,2},{1,3},{2,0},{3,1},{4,6},{5,7},{6,4},{7,5},{8,10},{9,11},{10,... | collective-permute-start | bytes 20 | tf_op jit(solution)/shard_map/ppermute | solution.py:432
  85.2 8.6 %collective-permute-start.21 = (bf16[384,512]{1,0:T(8,128)(2,1)S(1)}, bf16[384,512]{1,0:T(8,128)(2,1)S(1)}, u32[]{:S(2)}, u32[]{:S(2)}) collective-permute-start(bf16[384,512]{1,0:T(8,128)(2,1)S(1)} %get-tuple-element.77.refs_0_), channel_id=1, source_target_pairs={{0,4},{4,0},{8,12},{12,8},{16,20},{20,16},{24,28},{28,24},{1,5},{5... | collective-permute-start | bytes 1179656 | tf_op jit(solution)/shard_map/ppermute | solution.py:49
  86.0 7.7 %collective-permute-start.22 = (bf16[384,512]{1,0:T(8,128)(2,1)S(1)}, bf16[384,512]{1,0:T(8,128)(2,1)S(1)}, u32[]{:S(2)}, u32[]{:S(2)}) collective-permute-start(bf16[384,512]{1,0:T(8,128)(2,1)S(1)} %get-tuple-element.78.refs_1_), channel_id=1, source_target_pairs={{0,4},{4,0},{8,12},{12,8},{16,20},{20,16},{24,28},{28,24},{1,5},{5... | collective-permute-start | bytes 1179656 | tf_op jit(solution)/shard_map/ppermute | solution.py:49
  86.1 14.0 %collective-permute-start.31 = (bf16[384,512]{1,0:T(8,128)(2,1)S(1)}, bf16[384,512]{1,0:T(8,128)(2,1)S(1)}, u32[]{:S(2)}, u32[]{:S(2)}) collective-permute-start(bf16[384,512]{1,0:T(8,128)(2,1)S(1)} %collective-permute-done.23.refs_8_), channel_id=1, source_target_pairs={{0,16},{4,20},{8,24},{12,28},{16,0},{20,4},{24,8},{28,12},{1,17},{... | collective-permute-start | bytes 1179656 | tf_op jit(solution)/shard_map/ppermute | solution.py:49
  90.8 10.5 %collective-permute-start.32 = (bf16[384,512]{1,0:T(8,128)(2,1)S(1)}, bf16[384,512]{1,0:T(8,128)(2,1)S(1)}, u32[]{:S(2)}, u32[]{:S(2)}) collective-permute-start(bf16[384,512]{1,0:T(8,128)(2,1)S(1)} %collective-permute-done.28.refs_17_), channel_id=1, source_target_pairs={{0,8},{4,12},{8,0},{12,4},{16,24},{20,28},{24,16},{28,20},{1,9},{5... | collective-permute-start | bytes 1179656 | tf_op jit(solution)/shard_map/ppermute | solution.py:49
  92.1 10.3 %collective-permute-start.25 = (bf16[384,512]{1,0:T(8,128)(2,1)S(1)}, bf16[384,512]{1,0:T(8,128)(2,1)S(1)}, u32[]{:S(2)}, u32[]{:S(2)}) collective-permute-start(bf16[384,512]{1,0:T(8,128)(2,1)S(1)} %collective-permute-done.23.refs_8_), channel_id=1, source_target_pairs={{0,4},{4,0},{8,12},{12,8},{16,20},{20,16},{24,28},{28,24},{1,5},{5... | collective-permute-start | bytes 1179656 | tf_op jit(solution)/shard_map/ppermute | solution.py:49
  93.8 11.9 %collective-permute-start.30 = (bf16[384,512]{1,0:T(8,128)(2,1)S(1)}, bf16[384,512]{1,0:T(8,128)(2,1)S(1)}, u32[]{:S(2)}, u32[]{:S(2)}) collective-permute-start(bf16[384,512]{1,0:T(8,128)(2,1)S(1)} %collective-permute-done.28.refs_17_), channel_id=1, source_target_pairs={{0,4},{4,0},{8,12},{12,8},{16,20},{20,16},{24,28},{28,24},{1,5},{5... | collective-permute-start | bytes 1179656 | tf_op jit(solution)/shard_map/ppermute | solution.py:49
  93.8 12.7 %collective-permute-start.26 = (bf16[384,512]{1,0:T(8,128)(2,1)S(1)}, bf16[384,512]{1,0:T(8,128)(2,1)S(1)}, u32[]{:S(2)}, u32[]{:S(2)}) collective-permute-start(bf16[384,512]{1,0:T(8,128)(2,1)S(1)} %collective-permute-done.24.refs_9_), channel_id=1, source_target_pairs={{0,4},{4,0},{8,12},{12,8},{16,20},{20,16},{24,28},{28,24},{1,5},{5... | collective-permute-start | bytes 1179656 | tf_op jit(solution)/shard_map/ppermute | solution.py:49
  100.1 7.2 %collective-permute-start.29 = (bf16[384,512]{1,0:T(8,128)(2,1)S(1)}, bf16[384,512]{1,0:T(8,128)(2,1)S(1)}, u32[]{:S(2)}, u32[]{:S(2)}) collective-permute-start(bf16[384,512]{1,0:T(8,128)(2,1)S(1)} %collective-permute-done.27.refs_16_), channel_id=1, source_target_pairs={{0,4},{4,0},{8,12},{12,8},{16,20},{20,16},{24,28},{28,24},{1,5},{5... | collective-permute-start | bytes 1179656 | tf_op jit(solution)/shard_map/ppermute | solution.py:49
  101.3 6.7 %copy-start.1 = (bf16[384,512]{1,0:T(8,128)(2,1)}, bf16[384,512]{1,0:T(8,128)(2,1)S(1)}, u32[]{:S(2)}) copy-start(bf16[384,512]{1,0:T(8,128)(2,1)S(1)} %collective-permute-done.32.refs_25_) | copy-start | bytes 1179652
  101.3 6.7 %collective-permute-start.33 = (bf16[384,512]{1,0:T(8,128)(2,1)S(1)}, bf16[384,512]{1,0:T(8,128)(2,1)S(1)}, u32[]{:S(2)}, u32[]{:S(2)}) collective-permute-start(bf16[384,512]{1,0:T(8,128)(2,1)S(1)} %collective-permute-done.31.refs_24_), channel_id=1, source_target_pairs={{0,4},{4,0},{8,12},{12,8},{16,20},{20,16},{24,28},{28,24},{1,5},{5... | collective-permute-start | bytes 1179656 | tf_op jit(solution)/shard_map/ppermute | solution.py:49
  103.2 5.6 %collective-permute-start.34 = (bf16[384,512]{1,0:T(8,128)(2,1)S(1)}, bf16[384,512]{1,0:T(8,128)(2,1)S(1)}, u32[]{:S(2)}, u32[]{:S(2)}) collective-permute-start(bf16[384,512]{1,0:T(8,128)(2,1)S(1)} %collective-permute-done.32.refs_25_), channel_id=1, source_target_pairs={{0,4},{4,0},{8,12},{12,8},{16,20},{20,16},{24,28},{28,24},{1,5},{5... | collective-permute-start | bytes 1179656 | tf_op jit(solution)/shard_map/ppermute | solution.py:49
  132.1 31.4 %collective-permute-start.37 = (bf16[160,512]{1,0:T(8,128)(2,1)}, bf16[160,512]{1,0:T(8,128)(2,1)}, u32[]{:S(2)}, u32[]{:S(2)}) collective-permute-start(bf16[160,512]{1,0:T(8,128)(2,1)} %get-tuple-element.112), channel_id=1, source_target_pairs={{0,4},{4,0},{8,12},{12,8},{16,20},{20,16},{24,28},{28,24},{1,5},{5... | collective-permute-start | bytes 491528 | tf_op jit(solution)/shard_map/ppermute | solution.py:49
  132.5 45.5 %copy-start.27 = (s32[1,160]{1,0:T(1,128)S(1)}, s32[1,160]{1,0:T(1,128)}, u32[]{:S(2)}) copy-start(s32[1,160]{1,0:T(1,128)} %mask_ref.3) | copy-start | bytes 1924
  132.5 33.0 %collective-permute-start.38 = (bf16[160,512]{1,0:T(8,128)(2,1)}, bf16[160,512]{1,0:T(8,128)(2,1)}, u32[]{:S(2)}, u32[]{:S(2)}) collective-permute-start(bf16[160,512]{1,0:T(8,128)(2,1)} %get-tuple-element.113), channel_id=1, source_target_pairs={{0,8},{4,12},{8,0},{12,4},{16,24},{20,28},{24,16},{28,20},{1,9},{5... | collective-permute-start | bytes 491528 | tf_op jit(solution)/shard_map/ppermute | solution.py:49
  142.0 18.2 %copy-start.37 = (bf16[160,512]{1,0:T(8,128)(2,1)S(1)}, bf16[160,512]{1,0:T(8,128)(2,1)}, u32[]{:S(2)}) copy-start(bf16[160,512]{1,0:T(8,128)(2,1)} %copy-done.36) | copy-start | bytes 491524
  142.0 19.6 %copy-start.35 = (bf16[160,512]{1,0:T(8,128)(2,1)S(1)}, bf16[160,512]{1,0:T(8,128)(2,1)}, u32[]{:S(2)}) copy-start(bf16[160,512]{1,0:T(8,128)(2,1)} %copy-done.34) | copy-start | bytes 491524
  142.0 21.2 %copy-start.33 = (bf16[160,512]{1,0:T(8,128)(2,1)S(1)}, bf16[160,512]{1,0:T(8,128)(2,1)}, u32[]{:S(2)}) copy-start(bf16[160,512]{1,0:T(8,128)(2,1)} %copy-done.32) | copy-start | bytes 491524
  142.0 21.5 %copy-start.31 = (bf16[160,512]{1,0:T(8,128)(2,1)S(1)}, bf16[160,512]{1,0:T(8,128)(2,1)}, u32[]{:S(2)}) copy-start(bf16[160,512]{1,0:T(8,128)(2,1)} %copy-done.30) | copy-start | bytes 491524
  142.0 23.6 %copy-start.29 = (bf16[160,512]{1,0:T(8,128)(2,1)S(1)}, bf16[160,512]{1,0:T(8,128)(2,1)}, u32[]{:S(2)}) copy-start(bf16[160,512]{1,0:T(8,128)(2,1)} %copy-done.28) | copy-start | bytes 491524
  142.0 36.1 %copy-start.26 = (bf16[160,512]{1,0:T(8,128)(2,1)S(1)}, bf16[160,512]{1,0:T(8,128)(2,1)}, u32[]{:S(2)}) copy-start(bf16[160,512]{1,0:T(8,128)(2,1)} %copy-done.25) | copy-start | bytes 491524
  151.8 2.2 %collective-permute-start.44 = (bf16[160,128]{1,0:T(8,128)(2,1)S(1)}, bf16[160,128]{1,0:T(8,128)(2,1)S(1)}, u32[]{:S(2)}, u32[]{:S(2)}) collective-permute-start(bf16[160,128]{1,0:T(8,128)(2,1)S(1)} %get-tuple-element.121), channel_id=1, source_target_pairs={{0,4},{4,0},{8,12},{12,8},{16,20},{20,16},{24,28},{28,24},{1,5},{5... | collective-permute-start | bytes 122888 | tf_op jit(solution)/shard_map/ppermute | solution.py:49
  152.2 3.1 %collective-permute-start.45 = (bf16[160,128]{1,0:T(8,128)(2,1)S(1)}, bf16[160,128]{1,0:T(8,128)(2,1)S(1)}, u32[]{:S(2)}, u32[]{:S(2)}) collective-permute-start(bf16[160,128]{1,0:T(8,128)(2,1)S(1)} %get-tuple-element.122), channel_id=1, source_target_pairs={{0,8},{4,12},{8,0},{12,4},{16,24},{20,28},{24,16},{28,20},{1,9},{5... | collective-permute-start | bytes 122888 | tf_op jit(solution)/shard_map/ppermute | solution.py:49
  152.4 5.4 %collective-permute-start.46 = (bf16[160,128]{1,0:T(8,128)(2,1)S(1)}, bf16[160,128]{1,0:T(8,128)(2,1)S(1)}, u32[]{:S(2)}, u32[]{:S(2)}) collective-permute-start(bf16[160,128]{1,0:T(8,128)(2,1)S(1)} %get-tuple-element.123), channel_id=1, source_target_pairs={{0,12},{4,8},{8,4},{12,0},{16,28},{20,24},{24,20},{28,16},{1,13},{... | collective-permute-start | bytes 122888 | tf_op jit(solution)/shard_map/ppermute | solution.py:49
  154.0 4.5 %collective-permute-start.47 = (bf16[160,128]{1,0:T(8,128)(2,1)S(1)}, bf16[160,128]{1,0:T(8,128)(2,1)S(1)}, u32[]{:S(2)}, u32[]{:S(2)}) collective-permute-start(bf16[160,128]{1,0:T(8,128)(2,1)S(1)} %get-tuple-element.124), channel_id=1, source_target_pairs={{0,16},{4,20},{8,24},{12,28},{16,0},{20,4},{24,8},{28,12},{1,17},{... | collective-permute-start | bytes 122888 | tf_op jit(solution)/shard_map/ppermute | solution.py:49
  155.2 5.0 %collective-permute-start.48 = (bf16[160,128]{1,0:T(8,128)(2,1)S(1)}, bf16[160,128]{1,0:T(8,128)(2,1)S(1)}, u32[]{:S(2)}, u32[]{:S(2)}) collective-permute-start(bf16[160,128]{1,0:T(8,128)(2,1)S(1)} %get-tuple-element.125), channel_id=1, source_target_pairs={{0,20},{4,16},{8,28},{12,24},{16,4},{20,0},{24,12},{28,8},{1,21},{... | collective-permute-start | bytes 122888 | tf_op jit(solution)/shard_map/ppermute | solution.py:49
  157.8 3.8 %collective-permute-start.49 = (bf16[160,128]{1,0:T(8,128)(2,1)S(1)}, bf16[160,128]{1,0:T(8,128)(2,1)S(1)}, u32[]{:S(2)}, u32[]{:S(2)}) collective-permute-start(bf16[160,128]{1,0:T(8,128)(2,1)S(1)} %get-tuple-element.126), channel_id=1, source_target_pairs={{0,24},{4,28},{8,16},{12,20},{16,8},{20,12},{24,0},{28,4},{1,25},{... | collective-permute-start | bytes 122888 | tf_op jit(solution)/shard_map/ppermute | solution.py:49
  158.5 4.6 %collective-permute-start.50 = (bf16[160,128]{1,0:T(8,128)(2,1)S(1)}, bf16[160,128]{1,0:T(8,128)(2,1)S(1)}, u32[]{:S(2)}, u32[]{:S(2)}) collective-permute-start(bf16[160,128]{1,0:T(8,128)(2,1)S(1)} %get-tuple-element.127), channel_id=1, source_target_pairs={{0,28},{4,24},{8,20},{12,16},{16,12},{20,8},{24,4},{28,0},{1,29},{... | collective-permute-start | bytes 122888 | tf_op jit(solution)/shard_map/ppermute | solution.py:49
  160.2 6.5 %collective-permute-start.39 = (bf16[160,512]{1,0:T(8,128)(2,1)S(1)}, bf16[160,512]{1,0:T(8,128)(2,1)S(1)}, u32[]{:S(2)}, u32[]{:S(2)}) collective-permute-start(bf16[160,512]{1,0:T(8,128)(2,1)S(1)} %copy-done.37), channel_id=1, source_target_pairs={{0,12},{4,8},{8,4},{12,0},{16,28},{20,24},{24,20},{28,16},{1,13},{... | collective-permute-start | bytes 491528 | tf_op jit(solution)/shard_map/ppermute | solution.py:49
  161.6 12.8 %collective-permute-start.40 = (bf16[160,512]{1,0:T(8,128)(2,1)S(1)}, bf16[160,512]{1,0:T(8,128)(2,1)S(1)}, u32[]{:S(2)}, u32[]{:S(2)}) collective-permute-start(bf16[160,512]{1,0:T(8,128)(2,1)S(1)} %copy-done.35), channel_id=1, source_target_pairs={{0,16},{4,20},{8,24},{12,28},{16,0},{20,4},{24,8},{28,12},{1,17},{... | collective-permute-start | bytes 491528 | tf_op jit(solution)/shard_map/ppermute | solution.py:49
  163.1 14.9 %collective-permute-start.41 = (bf16[160,512]{1,0:T(8,128)(2,1)S(1)}, bf16[160,512]{1,0:T(8,128)(2,1)S(1)}, u32[]{:S(2)}, u32[]{:S(2)}) collective-permute-start(bf16[160,512]{1,0:T(8,128)(2,1)S(1)} %copy-done.33), channel_id=1, source_target_pairs={{0,20},{4,16},{8,28},{12,24},{16,4},{20,0},{24,12},{28,8},{1,21},{... | collective-permute-start | bytes 491528 | tf_op jit(solution)/shard_map/ppermute | solution.py:49
  163.5 14.6 %collective-permute-start.42 = (bf16[160,512]{1,0:T(8,128)(2,1)S(1)}, bf16[160,512]{1,0:T(8,128)(2,1)S(1)}, u32[]{:S(2)}, u32[]{:S(2)}) collective-permute-start(bf16[160,512]{1,0:T(8,128)(2,1)S(1)} %copy-done.31), channel_id=1, source_target_pairs={{0,24},{4,28},{8,16},{12,20},{16,8},{20,12},{24,0},{28,4},{1,25},{... | collective-permute-start | bytes 491528 | tf_op jit(solution)/shard_map/ppermute | solution.py:49
  165.6 12.5 %collective-permute-start.43 = (bf16[160,512]{1,0:T(8,128)(2,1)S(1)}, bf16[160,512]{1,0:T(8,128)(2,1)S(1)}, u32[]{:S(2)}, u32[]{:S(2)}) collective-permute-start(bf16[160,512]{1,0:T(8,128)(2,1)S(1)} %copy-done.29), channel_id=1, source_target_pairs={{0,28},{4,24},{8,20},{12,16},{16,12},{20,8},{24,4},{28,0},{1,29},{... | collective-permute-start | bytes 491528 | tf_op jit(solution)/shard_map/ppermute | solution.py:49
  (29 other events, 28.5 us)
Sparse Core Ops, SparseCore 0:
  12.4 79.4 all-gather.2
  93.4 28.7 all-gather.4
